TPU v7x, 32 devices: a whole 2x2x4 slice. The times are simulated.
32 devices in a mesh: dp: 8 (over z, y), tensor: 4 (over x, core).
Axes of the slice: x: 2, y: 2, z: 4, core: 2. Of those that a mesh axis runs over, the one named last changes fastest.
Arguments:
- d_out: bfloat16 [4096, 2560], P(('dp', 'tensor')), may hold values from -2.5 to 2.5
- gate_pre: bfloat16 [4096, 7168], P('dp', 'tensor'), may hold values from -6 to 6
- up_pre: bfloat16 [4096, 7168], P('dp', 'tensor'), may hold values from -40 to 40
- w_down: float32 [2560, 7168], P('dp', 'tensor'), may hold values from -280 to 280
- momentum: float32 [2560, 7168], P('dp', 'tensor'), may hold values from -3 to 3
Outputs:
- d_gate: bfloat16 [4096, 7168], P('dp', 'tensor')
- d_up: bfloat16 [4096, 7168], P('dp', 'tensor')
- w_new: float32 [2560, 7168], P('dp', 'tensor')
- momentum_new: float32 [2560, 7168], P('dp', 'tensor')
All inputs are finite; a program needn't handle non-finite values.
Results may differ from a plain program's by a relative error of at most 0.0049.
Values may be sent and summed in bfloat16 or wider, within the bound.
No kernel may reach another device: no remote copies, remote signals or barrier semaphores. Data moves between devices by JAX's collectives and lax.ppermute only.
A program may use at most 128 MiB of HBM per device.

v0:
```python
import jax
import jax.numpy as jnp
from jax import lax
from jax.sharding import PartitionSpec as P

FF = 7168


def body(d_out, gate_pre, up_pre, w_down, momentum):
    multiplier = FF ** (-0.5)
    gate_value = gate_pre.astype(jnp.float32)
    up_value = up_pre.astype(jnp.float32)
    sigmoid_gate = jax.nn.sigmoid(gate_value)
    hidden = (gate_value * sigmoid_gate * up_value).astype(jnp.bfloat16)
    group_out = lax.all_gather(d_out, "tensor", axis=0, tiled=True)
    w_low = w_down.astype(jnp.bfloat16)
    w_full = lax.all_gather(w_low, "dp", axis=0, tiled=True)
    d_hidden = jnp.dot(group_out, w_full, preferred_element_type=jnp.float32) * multiplier
    grad_local = (
        lax.dot_general(
            group_out, hidden, (((0,), (0,)), ((), ())), preferred_element_type=jnp.float32
        )
        * multiplier
    )
    grad = lax.psum_scatter(grad_local, "dp", scatter_dimension=0, tiled=True)
    d_gate = (
        d_hidden * up_value * sigmoid_gate * (1.0 + gate_value * (1.0 - sigmoid_gate))
    ).astype(jnp.bfloat16)
    d_up = (d_hidden * gate_value * sigmoid_gate).astype(jnp.bfloat16)
    weight_square = jnp.sum(w_down * w_down, axis=1, keepdims=True)
    grad_square = jnp.sum(grad * grad, axis=1, keepdims=True)
    weight_square, grad_square = lax.psum((weight_square, grad_square), "tensor")
    factor = jnp.minimum(1.0, 0.1 * jnp.sqrt(weight_square) / jnp.sqrt(grad_square + 1e-06))
    momentum_new = 0.9 * momentum + grad * factor
    w_new = w_down - 0.05 * momentum_new
    return (d_gate, d_up, w_new, momentum_new)


def solution(mesh):
    placed = (
        P(("dp", "tensor"), None),
        P("dp", "tensor"),
        P("dp", "tensor"),
        P("dp", "tensor"),
        P("dp", "tensor"),
    )
    return jax.shard_map(
        body,
        mesh=mesh,
        in_specs=placed,
        out_specs=(P("dp", "tensor"), P("dp", "tensor"), P("dp", "tensor"), P("dp", "tensor")),
        check_vma=False,
    )
```

profile of v0, /device:TPU:0, one launch (start us, length us, event | category | flops | bytes accessed | tf_op | source)
XLA Modules:
  0.0 510.3 jit_solution(10141494386778281710)
XLA Ops:
  7.2 0.0 copy-start.3
  7.2 0.0 all-gather.3.cloned.1.call-start
  7.2 0.7 all-gather.3.cloned.1.call-update
  7.9 0.0 all-gather.5.cloned.1.call-start
  8.0 3.6 multiply_reduce_fusion.1
  11.6 0.0 all-gather.5.cloned.1.call-update
  11.6 0.0 reduce-scatter.4.cloned.1.call-start
  11.7 26.2 %all-gather.3.cloned.1.call-done = bf16[512,2560]{1,0:T(8,128)(2,1)} async-done(((bf16[128,2560]{1,0:T(8,128)(2,1)}), bf16[512,2560]{1,0:T(8,128)(2,1)}) %all-gather.3.cloned.1.call-update) | async-done | bytes 2621456 | tf_op jit(solution)/shard_map/all_gather | solution.py:15
  37.9 0.0 copy-done.3
  37.9 14.9 %multiply_bitcast_fusion = f32[2560,1792]{0,1:T(8,128)} fusion(bf16[512,2560]{1,0:T(8,128)(2,1)} %all-gather.3.cloned.1.call-done, bf16[512,1792]{1,0:T(8,128)(2,1)} %param.7, bf16[512,1792]{1,0:T(8,128)(2,1)S(1)} %copy-done.3), kind=kOutput, calls=%fused_computation | convolution fusion | flops 4709548032 | bytes 24641536 | tf_op jit(solution)/shard_map/dot_general | solution.py:20
  52.8 19.4 %copy.21 = f32[2560,1792]{1,0:T(8,128)} copy(f32[2560,1792]{0,1:T(8,128)} %multiply_bitcast_fusion) | data formatting | bytes 36700160
  72.1 0.0 reduce-scatter.4.cloned.1.call-update
  72.2 1.6 copy-done.1
  73.8 2.2 copy.18
  75.9 3.4 copy.17
  79.4 96.2 %all-gather.5.cloned.1.call-done = bf16[2560,1792]{1,0:T(8,128)(2,1)} async-done(((bf16[320,1792]{1,0:T(8,128)(2,1)}), bf16[2560,1792]{1,0:T(8,128)(2,1)}) %all-gather.5.cloned.1.call-update) | async-done | bytes 9175056 | tf_op jit(solution)/shard_map/all_gather | solution.py:17
  175.5 11.3 %fusion.9 = (bf16[512,1792]{1,0:T(8,128)(2,1)}, bf16[512,1792]{1,0:T(8,128)(2,1)}) fusion(bf16[512,1792]{1,0:T(8,128)(2,1)} %param.6, bf16[512,1792]{1,0:T(8,128)(2,1)} %param.7, bf16[512,2560]{1,0:T(8,128)(2,1)S(1)} %copy-done.2, bf16[2560,1792]{1,0:T(8,128)(2,1)} %all-gather.5.cloned.1.call-done), kind=kOutput, calls=%fused_computation.16 | convolution fusion | flops 4712300544 | bytes 19136512 | tf_op jit(solution)/shard_map/dot_general | solution.py:18
  186.8 296.6 %reduce-scatter.4.cloned.1.call-done = f32[320,1792]{1,0:T(8,128)} async-done(((f32[2560,1792]{1,0:T(8,128)}), f32[320,1792]{1,0:T(8,128)}) %reduce-scatter.4.cloned.1.call-update) | async-done | bytes 2293776
  483.5 2.1 copy.22
  485.6 0.3 multiply_reduce_fusion
  485.9 6.8 %all-reduce = (f32[320,1]{0,1:T(1,128)S(1)}, f32[320,1]{0,1:T(1,128)S(1)}) all-reduce(f32[320,1]{0,1:T(1,128)S(1)} %broadcast_in_dim.7, f32[320,1]{0,1:T(1,128)S(1)} %broadcast_in_dim.6), channel_id=1, replica_groups=mesh['dp'=8,'tensor'=4] {'tensor'}, use_global_device_ids=true, to_apply=%region_4.0 | all-reduce | flops 640 | bytes 5120 | tf_op jit(solution)/shard_map/psum | solution.py:32
  492.8 5.6 %multiply_subtract_fusion = (f32[320,1792]{0,1:T(8,128)}, f32[320,1792]{0,1:T(8,128)}) fusion(f32[320,1792]{0,1:T(8,128)} %copy.18, f32[320,1792]{0,1:T(8,128)S(1)} %copy.22, f32[320]{0:T(512)S(1)} %minimum_reduce_fusion, f32[320,1792]{0,1:T(8,128)} %copy.17), kind=kLoop, calls=%fused_computation.17 | loop fusion | flops 2867200 | bytes 11470080 | tf_op jit(solution)/shard_map/sub | solution.py:35
  498.4 3.3 copy.19
  501.7 2.0 copy.20
  (8 shorter events, 0.0 us)
Async XLA Ops:
  7.2 30.7 %copy-start.3 = (bf16[512,1792]{1,0:T(8,128)(2,1)S(1)}, bf16[512,1792]{1,0:T(8,128)(2,1)}, u32[]{:S(2)}) copy-start(bf16[512,1792]{1,0:T(8,128)(2,1)} %param.6) | copy-start | bytes 5505028
  7.2 30.7 %all-gather.3.cloned.1.call-start = ((), (), s32[]{:S(2)}) async-start(), calls=%async_computation.1 | async-start | bytes 3276800 | tf_op jit(solution)/shard_map/all_gather | solution.py:15
  7.9 167.6 %all-gather.5.cloned.1.call-start = ((), (), s32[]{:S(2)}) async-start(), calls=%async_computation.2 | async-start | bytes 10321920 | tf_op jit(solution)/shard_map/all_gather | solution.py:17
  11.6 471.9 %reduce-scatter.4.cloned.1.call-start = ((), (), s32[]{:S(2)}) async-start(), calls=%async_computation.3 | async-start | bytes 20643840
  72.1 1.6 copy-start.1
  75.9 99.6 %copy-start.2 = (bf16[512,2560]{1,0:T(8,128)(2,1)S(1)}, bf16[512,2560]{1,0:T(8,128)(2,1)}, u32[]{:S(2)}) copy-start(bf16[512,2560]{1,0:T(8,128)(2,1)} %all-gather.3.cloned.1.call-done) | copy-start | bytes 7864324
  498.4 3.3 copy-start
Sparse Core Ops, SparseCore 0:
  9.6 28.2 all-gather.2
  40.6 134.8 all-gather.4
  179.5 303.9 reduce-scatter.3
where the time goes:
time: 511 us; the launch traced here: 510 us
  waiting for transfers between devices  420 us (82%)
  local copies, waits for them, and re-layouts  34.1 us (7%)
  matrix products  26.2 us (5%)
  between operations  13.8 us (3%)
  other arithmetic  9.55 us (2%)
  blocking collectives  6.84 us (1%)
    unnamed x4, waiting for transfers between devices  297 us
    all_gather x1, waiting for transfers between devices, body(): w_full = lax.all_gather(w_low, 'dp', axis=0, tiled=True)  96.2 us
    unnamed x14, local copies, waits for them, and re-layouts  34.1 us
    all_gather x1, waiting for transfers between devices, body(): group_out = lax.all_gather(d_out, 'tensor', axis=0, tiled=True)  26.2 us
    dot_general x1, matrix products, body(): lax.dot_general(group_out, hidden, (((0,), (0,)), ((), ())), preferred_el...  14.9 us
    dot_general x1, matrix products, body(): jnp.dot(group_out, w_full, preferred_element_type=jnp.float32) * multiplier  11.3 us
  transfers between devices with their start and end apart: 3, of which 3 were waited for; matrix products, arithmetic and copies ran while one was open for 11% of the time, Pallas kernels for 0%

commit v1 on v0

v1 whole, which is shorter than its diff:
```python
import jax
import jax.numpy as jnp
from jax import lax
from jax.sharding import Mesh, PartitionSpec as P

FF = 7168
SWAP = [(0, 1), (1, 0)]
ORDER = {
    "own w": ["give w"],
    "over x": ["give w"],
    "hidden": ["own w"],
    "own half 1": ["give w"],
    "give a": ["over y 1", "shard"],
    "own half 2": ["hidden over y a"],
    "give b": ["over y 2", "partial 1a"],
    "gather 2E": ["send 1Ea"],
    "gather 2O": ["send 1Ea"],
    "mine b": ["gather 2E"],
    "send 1Eb": ["send 2Oa"],
    "send 2Ea": ["send 1Ea"],
    "send 2Oa": ["send 2Ea"],
    "gather 3E": ["send 1Eb"],
    "send 2Eb": ["gather 3E", "w squares"],
    "send 2Ob": ["send 2Eb"],
    "send 3Ea": ["send 2Ob"],
    "send 3Oa": ["send 3Ea"],
    "send 3Eb": ["back", "send 3Oa"],
    "send 3Ob": ["send 3Eb"],
    "grad a": ["send 3Ob"],
    "grad b": ["outputs"],
    "w squares": ["hidden over y a"],
    "diagonal 2": ["partial 1a"],
    "other 2": ["partial 1a"],
    "diagonal 1": ["shard"],
    "other 1": ["shard"],
}


def plane_sum(value):
    k = lax.axis_size("x") * 2
    across = [(i, k - 1 - i) for i in range(k)]
    return (
        value
        + lax.ppermute(value, "x", SWAP)
        + lax.ppermute(value, "c", SWAP)
        + lax.ppermute(value, ("x", "c"), across)
    )


def edges(n, parity, upward, downward):
    pairs = [(i, i + 1) for i in upward if i % 2 == parity]
    return pairs + [(i, i - 1) for i in downward if (i - 1) % 2 == parity]


class Graph:
    def __init__(self):
        self.rules, self.values, self.open = {}, {}, set()

    def rule(self, name, operand, work):
        self.rules[name] = (operand, work)

    def __getitem__(self, name):
        if name in self.values:
            return self.values[name]
        if name in self.open:
            raise ValueError("cycle at " + name)
        self.open.add(name)
        operand, work = self.rules[name]
        first = operand()
        waits = [self[other] for other in ORDER.get(name, ()) if other in self.rules]
        if waits:
            first = lax.optimization_barrier((first, waits))[0]
        self.values[name] = work(first)
        return self.values[name]


def body(d_out, gate_pre, up_pre, w_down, momentum):
    multiplier = FF ** (-0.5)
    n = lax.axis_size("z")
    z, y, x, c = (lax.axis_index(a) for a in ("z", "y", "x", "c"))
    rows = w_down.shape[0]
    height = 2 * rows
    cols = w_down.shape[1] // 2
    first = -(-cols // 256) * 128
    parts = {"a": (0, first), "b": (first, cols - first)}
    block, depth = d_out.shape
    half = n // 2 * height
    near_start = jnp.where(z < n // 2, depth - half, 0)
    starts = {"1": near_start, "2": depth - half - near_start}
    g = Graph()

    def in_order(a, b, axis):
        return jnp.where(
            y == 0, jnp.concatenate([a, b], axis=axis), jnp.concatenate([b, a], axis=axis)
        )

    def columns(a, start, width):
        return lax.dynamic_slice_in_dim(a, start, width, 1)

    def over(axis):
        return lambda value: lax.ppermute(value, axis, SWAP)

    def same(value):
        return value

    def weights(whose):
        return lambda w: columns(w, whose * cols, cols).astype(jnp.bfloat16)

    g.rule("give w", lambda: w_down, weights(1 - y))
    g.rule("own w", lambda: w_down, weights(y))
    g.rule("partner w", lambda: g["give w"], over("y"))
    g.rule("shard", lambda: in_order(g["own w"], g["partner w"], 0), same)
    g.rule("w squares", lambda: w_down, lambda w: jnp.sum(w * w, axis=1))

    def gather_pairs(s, parity):
        return edges(n, parity, range(s - 1, n - 1), range(1, n - s + 1))

    def gather(s, parity):
        pairs = gather_pairs(s, parity)
        if not pairs:
            return
        name, other = f"gather {s}{'EO'[parity]}", f"got {s - 1}{'OE'[parity]}"
        g.rule(name, (lambda: g["shard"]) if s == 1 else (lambda: g[other]), same)
        got = f"got {s}{'EO'[parity]}"
        g.rule(got, lambda: g[name], lambda v: lax.ppermute(v, "z", pairs))

    for s in range(1, n):
        gather(s, 0)
        gather(s, 1)

    def hidden(operands):
        gate, up = (v.astype(jnp.float32) for v in operands)
        return (gate * jax.nn.sigmoid(gate) * up).astype(jnp.bfloat16)

    g.rule("hidden", lambda: (gate_pre, up_pre), hidden)

    def hidden_part(p):
        start, width = parts[p]
        g.rule("mine " + p, lambda: columns(g["hidden"], y * cols + start, width), same)
        g.rule("give " + p, lambda: columns(g["hidden"], (1 - y) * cols + start, width), same)
        g.rule("hidden over y " + p, lambda: g["give " + p], over("y"))

    hidden_part("a")
    hidden_part("b")

    def arrange(operands):
        pair = jnp.concatenate(operands, axis=0)
        other = lax.ppermute(pair, "c", SWAP)
        out = jnp.zeros((4 * block, pair.shape[1]), pair.dtype)
        for source, core in ((pair, c), (other, 1 - c)):
            for k, chip in ((0, x), (1, 1 - x)):
                piece = source[k * block : (k + 1) * block]
                out = lax.dynamic_update_slice_in_dim(out, piece, (chip * 2 + core) * block, 0)
        return out

    g.rule("over x", lambda: d_out, over("x"))
    g.rule("group", lambda: (d_out, g["over x"]), arrange)

    def cotangents(k):
        g.rule("own half " + k, lambda: columns(d_out, starts[k], half), same)
        g.rule("over y " + k, lambda: g["own half " + k], over("y"))
        g.rule("diagonal " + k, lambda: g["over y " + k], over("x"))
        g.rule("other " + k, lambda: (g["over y " + k], g["diagonal " + k]), arrange)

    cotangents("1")
    cotangents("2")

    contract = (((0,), (0,)), ((), ()))

    def product(k, p):
        def work(mine):
            partial = lax.dot_general(
                columns(g["group"], starts[k], half),
                mine,
                contract,
                preferred_element_type=jnp.float32,
            ) + lax.dot_general(
                g["other " + k],
                g["hidden over y " + p],
                contract,
                preferred_element_type=jnp.float32,
            )
            return (partial * multiplier).astype(jnp.bfloat16)

        g.rule(f"partial {k}{p}", lambda: g["mine " + p], work)

    for k in starts:
        for p in parts:
            product(k, p)

    def chunk(p, k, s):
        k = jnp.clip(k, 0, n - 1) * height
        at = jnp.clip(k - starts["1"], 0, half - height)
        a = lax.dynamic_slice_in_dim(g["partial 1" + p], at, height, 0)
        if s <= n // 2:
            return a
        at = jnp.clip(k - starts["2"], 0, half - height)
        b = lax.dynamic_slice_in_dim(g["partial 2" + p], at, height, 0)
        return jnp.where((k >= starts["1"]) & (k < starts["1"] + half), a, b)

    def reduce(s, p, parity):
        pairs = edges(n, parity, range(0, s), range(n - s, n))
        if not pairs:
            return
        name, before = f"{s}{'EO'[parity]}{p}", f"{s - 1}{'OE'[parity]}{p}"

        def operand():
            value = chunk(p, jnp.where(z % 2 == parity, n - s + z, s - n + z), s)
            if "sum " + before not in g.rules:
                return value
            got = g["sum " + before]
            return (value.astype(jnp.float32) + got.astype(jnp.float32)).astype(value.dtype)

        g.rule("send " + name, operand, same)
        g.rule("sum " + name, lambda: g["send " + name], lambda v: lax.ppermute(v, "z", pairs))

    for s in range(1, n):
        for p in parts:
            reduce(s, p, 0)
            reduce(s, p, 1)

    def d_hidden_of(tokens):
        total = jnp.dot(
            columns(tokens, z * height, height), g["shard"], preferred_element_type=jnp.float32
        )
        for t in range(1, n):
            piece, place = g[f"got {t}E"], jnp.where(z % 2 == 0, z + t, z - t)
            if f"got {n - t}O" in g.rules:
                piece = jnp.where((place >= 0) & (place < n), piece, g[f"got {n - t}O"])
            total = total + jnp.dot(
                columns(tokens, place % n * height, height),
                piece,
                preferred_element_type=jnp.float32,
            )
        return (total * multiplier).astype(jnp.bfloat16)

    def other_tokens():
        a, b = g["other 1"], g["other 2"]
        return jnp.where(
            near_start == 0, jnp.concatenate([a, b], axis=1), jnp.concatenate([b, a], axis=1)
        )

    g.rule("back", other_tokens, d_hidden_of)
    g.rule("back over y", lambda: g["back"], over("y"))
    g.rule("here", lambda: g["group"], d_hidden_of)

    def gate_and_up(operands):
        gate, up = (v.astype(jnp.float32) for v in operands)
        d_hidden = in_order(g["here"], g["back over y"], 1).astype(jnp.float32)
        s = jax.nn.sigmoid(gate)
        d_gate = (d_hidden * up * s * (1.0 + gate * (1.0 - s))).astype(jnp.bfloat16)
        return d_gate, (d_hidden * gate * s).astype(jnp.bfloat16)

    g.rule("outputs", lambda: lax.optimization_barrier((gate_pre, up_pre, g["hidden"]))[:2], gate_and_up)

    def total(p):
        def work(even):
            whole = chunk(p, z, n).astype(jnp.float32) + even.astype(jnp.float32)
            return whole + g[f"sum {n - 1}O{p}"].astype(jnp.float32)

        g.rule("grad " + p, lambda: g[f"sum {n - 1}E{p}"], work)

        def rows_of(whose):
            low = g["grad " + p].astype(jnp.bfloat16)
            return lax.dynamic_slice_in_dim(low, whose * rows, rows, 0)

        g.rule("give grad " + p, lambda: rows_of(1 - y), same)
        g.rule("grad over y " + p, lambda: g["give grad " + p], over("y"))
        g.rule("keep grad " + p, lambda: rows_of(y), same)

    for p in parts:
        total(p)

    grad_square = sum(jnp.sum(g["grad " + p] * g["grad " + p], axis=1) for p in parts)
    keep = lax.dynamic_slice_in_dim(grad_square, y * rows, rows, 0)
    give = lax.dynamic_slice_in_dim(grad_square, (1 - y) * rows, rows, 0)
    grad_square = keep + lax.ppermute(give, "y", SWAP)
    squares = plane_sum(jnp.stack([g["w squares"], grad_square]))
    factor = jnp.minimum(1.0, 0.1 * jnp.sqrt(squares[0]) / jnp.sqrt(squares[1] + 1e-06))
    grad = in_order(
        jnp.concatenate([g["keep grad " + p] for p in parts], 1),
        jnp.concatenate([g["grad over y " + p] for p in parts], 1),
        1,
    ).astype(jnp.float32)
    momentum_new = 0.9 * momentum + grad * factor[:, None]
    w_new = w_down - 0.05 * momentum_new
    d_gate, d_up = g["outputs"]
    return (d_gate, d_up, w_new, momentum_new)


def solution(mesh):
    groups, parts = mesh.devices.shape
    fine = Mesh(mesh.devices.reshape(groups // 2, 2, parts // 2, 2), ("z", "y", "x", "c"))
    dp, tensor = ("z", "y"), ("x", "c")
    placed = P(dp, tensor)
    return jax.shard_map(
        body,
        mesh=fine,
        in_specs=(P(dp + tensor, None), placed, placed, placed, placed),
        out_specs=(placed,) * 4,
        check_vma=False,
    )
```

time: 511 us -> 151 us (0.30)
  waiting for transfers between devices: 420 us -> 49.4 us
  starting transfers between devices: 0.12 us -> 50.8 us
  local copies, waits for them, and re-layouts: 34.1 us -> 16.3 us
  between operations: 13.8 us -> 1.21 us
  matrix products: 26.2 us -> 15 us
  other arithmetic: 9.55 us -> 17.8 us
  blocking collectives: 6.84 us -> 0 us
    unnamed x4 -> x0, waiting for transfers between devices: 297 us -> none
    all_gather x2 -> x0, waiting for transfers between devices: 122 us -> none  [the longest x1 96.2 us: body(): w_full = lax.all_gather(w_low, 'dp', axis=0, tiled=True)]
    ppermute x0 -> x33, starting transfers between devices: none -> 50.8 us  [the longest x10 22.6 us: reduce(): lax.ppermute(v, 'z', pairs)]
    ppermute x0 -> x33, waiting for transfers between devices: none -> 49.4 us  [the longest x10 19.6 us: reduce(): lax.ppermute(v, 'z', pairs)]
    unnamed x14 -> x20, local copies, waits for them, and re-layouts: 34.1 us -> 3.23 us
    dot_general x2 -> x16, matrix products: 26.2 us -> 15 us  [the longest x6 6.05 us: d_hidden_of(): jnp.dot(columns(tokens, place % n * height, height), piece, preferred_ele...]
    convert_element_type x0 -> x8, other arithmetic: none -> 10.4 us  [the longest x1 3.84 us: hidden(): return (gate * jax.nn.sigmoid(gate) * up).astype(jnp.bfloat16)]
    psum x1 -> x0, blocking collectives: 6.84 us -> none  [body(): lax.psum((weight_square, grad_square), 'tensor')]
  transfers between devices with their start and end apart: 3 -> 33, of which waited for: 3 -> 13; matrix products, arithmetic and copies ran while one was open for 11% -> 27% of each run, Pallas kernels for 0% -> 0%
where the time goes in v1:
time: 151 us
  starting transfers between devices  50.8 us (34%)
  waiting for transfers between devices  49.4 us (33%)
  other arithmetic  17.8 us (12%)
  local copies, waits for them, and re-layouts  16.3 us (11%)
  matrix products  15 us (10%)
    ppermute x10, starting transfers between devices, reduce(): lax.ppermute(v, 'z', pairs)  22.6 us
    ppermute x10, waiting for transfers between devices, reduce(): lax.ppermute(v, 'z', pairs)  19.6 us
    ppermute x11, starting transfers between devices, over(): return lambda value: lax.ppermute(value, axis, SWAP)  15.4 us
    ppermute x5, waiting for transfers between devices, gather(): g.rule(got, lambda: g[name], lambda v: lax.ppermute(v, 'z', pairs))  14.8 us
    ppermute x11, waiting for transfers between devices, over(): return lambda value: lax.ppermute(value, axis, SWAP)  12.5 us
    ppermute x5, starting transfers between devices, gather(): g.rule(got, lambda: g[name], lambda v: lax.ppermute(v, 'z', pairs))  8.84 us
    dot_general x6, matrix products, d_hidden_of(): jnp.dot(columns(tokens, place % n * height, height), piece, preferred_ele...  6.05 us
    dynamic_slice x3, local copies, waits for them, and re-layouts, columns(): return lax.dynamic_slice_in_dim(a, start, width, 1)  5.11 us
  transfers between devices with their start and end apart: 33, of which 13 were waited for; matrix products, arithmetic and copies ran while one was open for 27% of the time, Pallas kernels for 0%

profile of v1, /device:TPU:0, one launch (start us, length us, event | category | flops | bytes accessed | tf_op | source)
XLA Modules:
  0.0 150.6 jit_solution(16002740624602400398)
XLA Ops:
  0.7 2.3 %dynamic-slice_convert_fusion.1 = bf16[320,896]{1,0:T(8,128)(2,1)} fusion(f32[320,1792]{1,0:T(8,128)} %param.8, s32[]{:T(128)S(6)} %select_n.261), kind=kLoop, calls=%fused_computation.52 | loop fusion | bytes 1146884 | tf_op jit(solution)/shard_map/convert_element_type | solution.py:107
  2.9 3.0 %collective-permute-start.2 = (bf16[320,896]{1,0:T(8,128)(2,1)}, bf16[320,896]{1,0:T(8,128)(2,1)}, u32[]{:S(2)}, u32[]{:S(2)}) collective-permute-start(bf16[320,896]{1,0:T(8,128)(2,1)} %dynamic-slice_convert_fusion.1), channel_id=1, source_target_pairs={{0,4},{4,0},{1,5},{5,1},{2,6},{6,2},{3,7},{7,3},{8,12},{12,8},{9,1... | collective-permute-start | bytes 1720328 | tf_op jit(solution)/shard_map/ppermute | solution.py:101
  7.4 1.9 %constant_dynamic-slice_fusion.7 = (bf16[128,1280]{1,0:T(8,128)(2,1)}, bf16[128,1280]{1,0:T(8,128)(2,1)}) fusion(bf16[128,2560]{1,0:T(8,128)(2,1)} %param.5, s32[]{:T(128)S(6)} %select_n.285, s32[]{:T(128)S(6)} %select_n.277), kind=kLoop, calls=%fused_computation.106 | loop fusion | bytes 1310728 | tf_op jit(solution)/shard_map/dynamic_slice | solution.py:98
  9.8 2.1 %dynamic-slice_convert_fusion = bf16[320,896]{1,0:T(8,128)(2,1)} fusion(f32[320,1792]{1,0:T(8,128)} %param.8, s32[]{:T(128)S(6)} %select_n.267), kind=kLoop, calls=%fused_computation.51 | loop fusion | bytes 1146884 | tf_op jit(solution)/shard_map/convert_element_type | solution.py:107
  12.0 3.8 %fusion.13 = bf16[512,1792]{1,0:T(8,128)(2,1)} fusion(bf16[512,1792]{1,0:T(8,128)(2,1)} %param.7, bf16[512,1792]{1,0:T(8,128)(2,1)S(1)} %copy-done.2), kind=kLoop, calls=%fused_computation.19 | loop fusion | flops 7340032 | bytes 5505024 | tf_op jit(solution)/shard_map/convert_element_type | solution.py:133
  16.9 1.9 %constant_dynamic-slice_fusion.11 = bf16[512,512]{1,0:T(8,128)(2,1)} fusion(bf16[512,1792]{1,0:T(8,128)(2,1)} %fusion.13, s32[]{:T(128)S(6)} %select_n.261), kind=kLoop, calls=%fused_computation.111 | loop fusion | bytes 1048580 | tf_op jit(solution)/shard_map/dynamic_slice | solution.py:98
  22.4 4.8 %collective-permute-start.3 = (bf16[640,896]{1,0:T(8,128)(2,1)S(1)}, bf16[640,896]{1,0:T(8,128)(2,1)S(1)}, u32[]{:S(2)}, u32[]{:S(2)}) collective-permute-start(bf16[640,896]{1,0:T(8,128)(2,1)S(1)} %maximum_select_fusion.2), channel_id=1, source_target_pairs={{0,8},{16,24},{8,0},{24,16},{1,9},{17,25},{9,1},{25,17},{2,10},{18... | collective-permute-start | bytes 3440648 | tf_op jit(solution)/shard_map/ppermute | solution.py:125
  32.7 2.6 %collective-permute-done.6 = bf16[128,1280]{1,0:T(8,128)(2,1)S(1)} collective-permute-done((bf16[128,1280]{1,0:T(8,128)(2,1)}, bf16[128,1280]{1,0:T(8,128)(2,1)S(1)}, u32[]{:S(2)}, u32[]{:S(2)}) %collective-permute-start.6) | collective-permute-done | bytes 327712 | tf_op jit(solution)/shard_map/ppermute | solution.py:101
  37.5 2.9 %collective-permute-done.8 = bf16[512,512]{1,0:T(8,128)(2,1)S(1)} collective-permute-done((bf16[512,512]{1,0:T(8,128)(2,1)S(1)}, bf16[512,512]{1,0:T(8,128)(2,1)S(1)}, u32[]{:S(2)}, u32[]{:S(2)}) %collective-permute-start.8) | collective-permute-done | bytes 524320 | tf_op jit(solution)/shard_map/ppermute | solution.py:101
  45.9 3.5 %collective-permute-start.13 = (bf16[640,512]{1,0:T(8,128)(2,1)S(1)}, bf16[640,512]{1,0:T(8,128)(2,1)S(1)}, u32[]{:S(2)}, u32[]{:S(2)}) collective-permute-start(bf16[640,512]{1,0:T(8,128)(2,1)S(1)} %get-tuple-element.83), channel_id=1, source_target_pairs={{0,8},{24,16},{1,9},{25,17},{2,10},{26,18},{3,11},{27,19},{4,12},{... | collective-permute-start | bytes 1966088 | tf_op jit(solution)/shard_map/ppermute | solution.py:215
  53.7 1.6 %collective-permute-start.12 = (bf16[512,384]{1,0:T(8,128)(2,1)S(1)}, bf16[512,384]{1,0:T(8,128)(2,1)S(1)}, u32[]{:S(2)}, u32[]{:S(2)}) collective-permute-start(bf16[512,384]{1,0:T(8,128)(2,1)S(1)} %get-tuple-element.49), channel_id=1, source_target_pairs={{0,4},{4,0},{1,5},{5,1},{2,6},{6,2},{3,7},{7,3},{8,12},{12,8},{9,1... | collective-permute-start | bytes 1179656 | tf_op jit(solution)/shard_map/ppermute | solution.py:101
  56.2 1.6 %collective-permute-done.15 = bf16[128,1280]{1,0:T(8,128)(2,1)S(1)} collective-permute-done((bf16[128,1280]{1,0:T(8,128)(2,1)S(1)}, bf16[128,1280]{1,0:T(8,128)(2,1)S(1)}, u32[]{:S(2)}, u32[]{:S(2)}) %collective-permute-start.15) | collective-permute-done | bytes 327712 | tf_op jit(solution)/shard_map/ppermute | solution.py:101
  57.9 4.6 %collective-permute-start.23 = (bf16[640,512]{1,0:T(8,128)(2,1)S(1)}, bf16[640,512]{1,0:T(8,128)(2,1)S(1)}, u32[]{:S(2)}, u32[]{:S(2)}) collective-permute-start(bf16[640,512]{1,0:T(8,128)(2,1)S(1)} %get-tuple-element.50), channel_id=1, source_target_pairs={{0,8},{24,16},{1,9},{25,17},{2,10},{26,18},{3,11},{27,19},{4,12},{... | collective-permute-start | bytes 1966088 | tf_op jit(solution)/shard_map/ppermute | solution.py:215
  64.9 2.1 %collective-permute-done.13 = bf16[640,512]{1,0:T(8,128)(2,1)S(1)} collective-permute-done((bf16[640,512]{1,0:T(8,128)(2,1)S(1)}, bf16[640,512]{1,0:T(8,128)(2,1)S(1)}, u32[]{:S(2)}, u32[]{:S(2)}) %collective-permute-start.13) | collective-permute-done | bytes 655392 | tf_op jit(solution)/shard_map/ppermute | solution.py:215
  68.0 5.8 %collective-permute-start.19 = (bf16[640,384]{1,0:T(8,128)(2,1)S(1)}, bf16[640,384]{1,0:T(8,128)(2,1)S(1)}, u32[]{:S(2)}, u32[]{:S(2)}) collective-permute-start(bf16[640,384]{1,0:T(8,128)(2,1)S(1)} %get-tuple-element.52), channel_id=1, source_target_pairs={{0,8},{24,16},{1,9},{25,17},{2,10},{26,18},{3,11},{27,19},{4,12},{... | collective-permute-start | bytes 1474568 | tf_op jit(solution)/shard_map/ppermute | solution.py:215
  81.3 7.5 %collective-permute-done.19 = bf16[640,384]{1,0:T(8,128)(2,1)S(1)} collective-permute-done((bf16[640,384]{1,0:T(8,128)(2,1)S(1)}, bf16[640,384]{1,0:T(8,128)(2,1)S(1)}, u32[]{:S(2)}, u32[]{:S(2)}) %collective-permute-start.19) | collective-permute-done | bytes 491552 | tf_op jit(solution)/shard_map/ppermute | solution.py:215
  89.1 4.4 %collective-permute-start.21 = (bf16[640,384]{1,0:T(8,128)(2,1)S(1)}, bf16[640,384]{1,0:T(8,128)(2,1)S(1)}, u32[]{:S(2)}, u32[]{:S(2)}) collective-permute-start(bf16[640,384]{1,0:T(8,128)(2,1)S(1)} %get-tuple-element.60), channel_id=1, source_target_pairs={{0,8},{24,16},{1,9},{25,17},{2,10},{26,18},{3,11},{27,19},{4,12},{... | collective-permute-start | bytes 1474568 | tf_op jit(solution)/shard_map/ppermute | solution.py:215
  98.9 14.1 %collective-permute-done.14 = bf16[640,896]{1,0:T(8,128)(2,1)S(1)} collective-permute-done((bf16[640,896]{1,0:T(8,128)(2,1)S(1)}, bf16[640,896]{1,0:T(8,128)(2,1)S(1)}, u32[]{:S(2)}, u32[]{:S(2)}) %collective-permute-start.14) | collective-permute-done | bytes 1146912 | tf_op jit(solution)/shard_map/ppermute | solution.py:125
  114.1 1.6 %collective-permute-start.17 = (bf16[512,896]{1,0:T(8,128)(2,1)S(1)}, bf16[512,896]{1,0:T(8,128)(2,1)S(1)}, u32[]{:S(2)}, u32[]{:S(2)}) collective-permute-start(bf16[512,896]{1,0:T(8,128)(2,1)S(1)} %multiply_convert_fusion), channel_id=1, source_target_pairs={{0,4},{4,0},{1,5},{5,1},{2,6},{6,2},{3,7},{7,3},{8,12},{12,8},{9,1... | collective-permute-start | bytes 2752520 | tf_op jit(solution)/shard_map/ppermute | solution.py:101
  117.3 9.7 %collective-permute-done.20 = bf16[640,512]{1,0:T(8,128)(2,1)S(1)} collective-permute-done((bf16[640,512]{1,0:T(8,128)(2,1)S(1)}, bf16[640,512]{1,0:T(8,128)(2,1)S(1)}, u32[]{:S(2)}, u32[]{:S(2)}) %collective-permute-start.20) | collective-permute-done | bytes 655392 | tf_op jit(solution)/shard_map/ppermute | solution.py:215
  129.7 3.4 %fusion.12 = (bf16[512,1792]{1,0:T(8,128)(2,1)}, bf16[512,1792]{1,0:T(8,128)(2,1)}) fusion(bf16[512,1792]{1,0:T(8,128)(2,1)S(1)} %copy-done.3, bf16[512,896]{1,0:T(8,128)(2,1)S(1)} %multiply_convert_fusion.1, bf16[512,896]{1,0:T(8,128)(2,1)S(1)} %collective-permute-done.17, pred[]{:T(512)S(6)} %eq.51, bf16[512,1792]{1,0:T(8,128)(2,1)S(1)} %copy-done.4), kind=kLoop, calls=%fused_computation.18 | loop fusion | flops 22937600 | bytes 9175041 | tf_op jit(solution)/shard_map/convert_element_type | solution.py:252
  140.0 1.6 %collective-permute-start.28 = (bf16[320,384]{1,0:T(8,128)(2,1)S(1)}, bf16[320,384]{1,0:T(8,128)(2,1)S(1)}, u32[]{:S(2)}, u32[]{:S(2)}) collective-permute-start(bf16[320,384]{1,0:T(8,128)(2,1)S(1)} %get-tuple-element.90), channel_id=1, source_target_pairs={{0,4},{4,0},{1,5},{5,1},{2,6},{6,2},{3,7},{7,3},{8,12},{12,8},{9,1... | collective-permute-start | bytes 737288 | tf_op jit(solution)/shard_map/ppermute | solution.py:101
  143.1 4.9 %collective-permute-done.28 = bf16[320,384]{1,0:T(8,128)(2,1)S(1)} collective-permute-done((bf16[320,384]{1,0:T(8,128)(2,1)S(1)}, bf16[320,384]{1,0:T(8,128)(2,1)S(1)}, u32[]{:S(2)}, u32[]{:S(2)}) %collective-permute-start.28) | collective-permute-done | bytes 245792 | tf_op jit(solution)/shard_map/ppermute | solution.py:101
  148.0 2.5 %multiply_subtract_fusion = (f32[320,1792]{1,0:T(8,128)}, f32[320,1792]{1,0:T(8,128)}) fusion(f32[320,1792]{1,0:T(8,128)S(1)} %copy-done, f32[320]{0:T(512)S(1)} %minimum_reduce_fusion, bf16[320,384]{1,0:T(8,128)(2,1)S(1)} %get-tuple-element.91, bf16[320,512]{1,0:T(8,128)(2,1)S(1)} %get-tuple-element.87, bf16[320,384]{1,0:T(8,128)(2,1)S(1)} %collective-permute-done.28, ...), kind=kLoop, calls=%fused_computation.33 | loop fusion | flops 13189120 | bytes 10323201 | tf_op jit(solution)/shard_map/sub | solution.py:286
  (125 shorter events, 54.9 us)
Async XLA Ops:
  2.9 17.2 %collective-permute-start.2 = (bf16[320,896]{1,0:T(8,128)(2,1)}, bf16[320,896]{1,0:T(8,128)(2,1)}, u32[]{:S(2)}, u32[]{:S(2)}) collective-permute-start(bf16[320,896]{1,0:T(8,128)(2,1)} %dynamic-slice_convert_fusion.1), channel_id=1, source_target_pairs={{0,4},{4,0},{1,5},{5,1},{2,6},{6,2},{3,7},{7,3},{8,12},{12,8},{9,1... | collective-permute-start | bytes 1720328 | tf_op jit(solution)/shard_map/ppermute | solution.py:101
  5.9 24.4 %collective-permute-start = (bf16[128,2560]{1,0:T(8,128)(2,1)}, bf16[128,2560]{1,0:T(8,128)(2,1)}, u32[]{:S(2)}, u32[]{:S(2)}) collective-permute-start(bf16[128,2560]{1,0:T(8,128)(2,1)} %param.5), channel_id=1, source_target_pairs={{0,2},{2,0},{1,3},{3,1},{4,6},{6,4},{5,7},{7,5},{8,10},{10,8},{9,1... | collective-permute-start | bytes 1966088 | tf_op jit(solution)/shard_map/ppermute | solution.py:101
  9.3 17.9 %collective-permute-start.5 = (bf16[128,1280]{1,0:T(8,128)(2,1)}, bf16[128,1280]{1,0:T(8,128)(2,1)}, u32[]{:S(2)}, u32[]{:S(2)}) collective-permute-start(bf16[128,1280]{1,0:T(8,128)(2,1)} %get-tuple-element.40), channel_id=1, source_target_pairs={{0,4},{4,0},{1,5},{5,1},{2,6},{6,2},{3,7},{7,3},{8,12},{12,8},{9,1... | collective-permute-start | bytes 983048 | tf_op jit(solution)/shard_map/ppermute | solution.py:101
  21.7 27.7 %collective-permute-start.4 = (bf16[640,896]{1,0:T(8,128)(2,1)S(1)}, bf16[640,896]{1,0:T(8,128)(2,1)S(1)}, u32[]{:S(2)}, u32[]{:S(2)}) collective-permute-start(bf16[640,896]{1,0:T(8,128)(2,1)S(1)} %maximum_select_fusion.2), channel_id=1, source_target_pairs={{8,16},{16,8},{9,17},{17,9},{10,18},{18,10},{11,19},{19,11},{12,20... | collective-permute-start | bytes 3440648 | tf_op jit(solution)/shard_map/ppermute | solution.py:125
  22.4 30.5 %collective-permute-start.3 = (bf16[640,896]{1,0:T(8,128)(2,1)S(1)}, bf16[640,896]{1,0:T(8,128)(2,1)S(1)}, u32[]{:S(2)}, u32[]{:S(2)}) collective-permute-start(bf16[640,896]{1,0:T(8,128)(2,1)S(1)} %maximum_select_fusion.2), channel_id=1, source_target_pairs={{0,8},{16,24},{8,0},{24,16},{1,9},{17,25},{9,1},{25,17},{2,10},{18... | collective-permute-start | bytes 3440648 | tf_op jit(solution)/shard_map/ppermute | solution.py:125
  27.3 8.0 %collective-permute-start.6 = (bf16[128,1280]{1,0:T(8,128)(2,1)}, bf16[128,1280]{1,0:T(8,128)(2,1)S(1)}, u32[]{:S(2)}, u32[]{:S(2)}) collective-permute-start(bf16[128,1280]{1,0:T(8,128)(2,1)} %collective-permute-done.5), channel_id=1, source_target_pairs={{0,2},{2,0},{1,3},{3,1},{4,6},{6,4},{5,7},{7,5},{8,10},{10,8},{9,1... | collective-permute-start | bytes 983048 | tf_op jit(solution)/shard_map/ppermute | solution.py:101
  28.7 11.7 %collective-permute-start.8 = (bf16[512,512]{1,0:T(8,128)(2,1)S(1)}, bf16[512,512]{1,0:T(8,128)(2,1)S(1)}, u32[]{:S(2)}, u32[]{:S(2)}) collective-permute-start(bf16[512,512]{1,0:T(8,128)(2,1)S(1)} %copy-done.8), channel_id=1, source_target_pairs={{0,4},{4,0},{1,5},{5,1},{2,6},{6,2},{3,7},{7,3},{8,12},{12,8},{9,1... | collective-permute-start | bytes 1572872 | tf_op jit(solution)/shard_map/ppermute | solution.py:101
  31.4 11.7 %collective-permute-start.1 = (bf16[256,2560]{1,0:T(8,128)(2,1)S(1)}, bf16[256,2560]{1,0:T(8,128)(2,1)S(1)}, u32[]{:S(2)}, u32[]{:S(2)}) collective-permute-start(bf16[256,2560]{1,0:T(8,128)(2,1)S(1)} %pad_maximum_fusion), channel_id=1, source_target_pairs={{0,1},{1,0},{2,3},{3,2},{4,5},{5,4},{6,7},{7,6},{8,9},{9,8},{10,11... | collective-permute-start | bytes 3932168 | tf_op jit(solution)/shard_map/ppermute | solution.py:148
  40.4 10.3 %collective-permute-start.11 = (bf16[128,1280]{1,0:T(8,128)(2,1)S(1)}, bf16[128,1280]{1,0:T(8,128)(2,1)S(1)}, u32[]{:S(2)}, u32[]{:S(2)}) collective-permute-start(bf16[128,1280]{1,0:T(8,128)(2,1)S(1)} %copy-done.9), channel_id=1, source_target_pairs={{0,4},{4,0},{1,5},{5,1},{2,6},{6,2},{3,7},{7,3},{8,12},{12,8},{9,1... | collective-permute-start | bytes 983048 | tf_op jit(solution)/shard_map/ppermute | solution.py:101
  45.9 21.1 %collective-permute-start.13 = (bf16[640,512]{1,0:T(8,128)(2,1)S(1)}, bf16[640,512]{1,0:T(8,128)(2,1)S(1)}, u32[]{:S(2)}, u32[]{:S(2)}) collective-permute-start(bf16[640,512]{1,0:T(8,128)(2,1)S(1)} %get-tuple-element.83), channel_id=1, source_target_pairs={{0,8},{24,16},{1,9},{25,17},{2,10},{26,18},{3,11},{27,19},{4,12},{... | collective-permute-start | bytes 1966088 | tf_op jit(solution)/shard_map/ppermute | solution.py:215
  49.4 44.1 %collective-permute-start.9 = (bf16[640,896]{1,0:T(8,128)(2,1)S(1)}, bf16[640,896]{1,0:T(8,128)(2,1)S(1)}, u32[]{:S(2)}, u32[]{:S(2)}) collective-permute-start(bf16[640,896]{1,0:T(8,128)(2,1)S(1)} %collective-permute-done.4), channel_id=1, source_target_pairs={{16,24},{8,0},{17,25},{9,1},{18,26},{10,2},{19,27},{11,3},{20,28},... | collective-permute-start | bytes 3440648 | tf_op jit(solution)/shard_map/ppermute | solution.py:125
  53.0 27.0 %collective-permute-start.10 = (bf16[640,896]{1,0:T(8,128)(2,1)S(1)}, bf16[640,896]{1,0:T(8,128)(2,1)S(1)}, u32[]{:S(2)}, u32[]{:S(2)}) collective-permute-start(bf16[640,896]{1,0:T(8,128)(2,1)S(1)} %collective-permute-done.3), channel_id=1, source_target_pairs={{8,16},{16,8},{9,17},{17,9},{10,18},{18,10},{11,19},{19,11},{12,20... | collective-permute-start | bytes 3440648 | tf_op jit(solution)/shard_map/ppermute | solution.py:125
  53.7 9.1 %collective-permute-start.12 = (bf16[512,384]{1,0:T(8,128)(2,1)S(1)}, bf16[512,384]{1,0:T(8,128)(2,1)S(1)}, u32[]{:S(2)}, u32[]{:S(2)}) collective-permute-start(bf16[512,384]{1,0:T(8,128)(2,1)S(1)} %get-tuple-element.49), channel_id=1, source_target_pairs={{0,4},{4,0},{1,5},{5,1},{2,6},{6,2},{3,7},{7,3},{8,12},{12,8},{9,1... | collective-permute-start | bytes 1179656 | tf_op jit(solution)/shard_map/ppermute | solution.py:101
  57.9 38.3 %collective-permute-start.23 = (bf16[640,512]{1,0:T(8,128)(2,1)S(1)}, bf16[640,512]{1,0:T(8,128)(2,1)S(1)}, u32[]{:S(2)}, u32[]{:S(2)}) collective-permute-start(bf16[640,512]{1,0:T(8,128)(2,1)S(1)} %get-tuple-element.50), channel_id=1, source_target_pairs={{0,8},{24,16},{1,9},{25,17},{2,10},{26,18},{3,11},{27,19},{4,12},{... | collective-permute-start | bytes 1966088 | tf_op jit(solution)/shard_map/ppermute | solution.py:215
  67.3 28.9 %collective-permute-start.18 = (bf16[640,512]{1,0:T(8,128)(2,1)S(1)}, bf16[640,512]{1,0:T(8,128)(2,1)S(1)}, u32[]{:S(2)}, u32[]{:S(2)}) collective-permute-start(bf16[640,512]{1,0:T(8,128)(2,1)S(1)} %add_convert_fusion.2), channel_id=1, source_target_pairs={{8,16},{16,8},{9,17},{17,9},{10,18},{18,10},{11,19},{19,11},{12,20... | collective-permute-start | bytes 1966088 | tf_op jit(solution)/shard_map/ppermute | solution.py:215
  68.0 20.9 %collective-permute-start.19 = (bf16[640,384]{1,0:T(8,128)(2,1)S(1)}, bf16[640,384]{1,0:T(8,128)(2,1)S(1)}, u32[]{:S(2)}, u32[]{:S(2)}) collective-permute-start(bf16[640,384]{1,0:T(8,128)(2,1)S(1)} %get-tuple-element.52), channel_id=1, source_target_pairs={{0,8},{24,16},{1,9},{25,17},{2,10},{26,18},{3,11},{27,19},{4,12},{... | collective-permute-start | bytes 1474568 | tf_op jit(solution)/shard_map/ppermute | solution.py:215
  80.0 33.0 %collective-permute-start.14 = (bf16[640,896]{1,0:T(8,128)(2,1)S(1)}, bf16[640,896]{1,0:T(8,128)(2,1)S(1)}, u32[]{:S(2)}, u32[]{:S(2)}) collective-permute-start(bf16[640,896]{1,0:T(8,128)(2,1)S(1)} %collective-permute-done.10), channel_id=1, source_target_pairs={{16,24},{8,0},{17,25},{9,1},{18,26},{10,2},{19,27},{11,3},{20,28},... | collective-permute-start | bytes 3440648 | tf_op jit(solution)/shard_map/ppermute | solution.py:125
  89.1 26.6 %collective-permute-start.21 = (bf16[640,384]{1,0:T(8,128)(2,1)S(1)}, bf16[640,384]{1,0:T(8,128)(2,1)S(1)}, u32[]{:S(2)}, u32[]{:S(2)}) collective-permute-start(bf16[640,384]{1,0:T(8,128)(2,1)S(1)} %get-tuple-element.60), channel_id=1, source_target_pairs={{0,8},{24,16},{1,9},{25,17},{2,10},{26,18},{3,11},{27,19},{4,12},{... | collective-permute-start | bytes 1474568 | tf_op jit(solution)/shard_map/ppermute | solution.py:215
  93.5 22.2 %collective-permute-start.22 = (bf16[640,384]{1,0:T(8,128)(2,1)S(1)}, bf16[640,384]{1,0:T(8,128)(2,1)S(1)}, u32[]{:S(2)}, u32[]{:S(2)}) collective-permute-start(bf16[640,384]{1,0:T(8,128)(2,1)S(1)} %add_convert_fusion.5), channel_id=1, source_target_pairs={{8,16},{16,8},{9,17},{17,9},{10,18},{18,10},{11,19},{19,11},{12,20... | collective-permute-start | bytes 1474568 | tf_op jit(solution)/shard_map/ppermute | solution.py:215
  97.1 29.9 %collective-permute-start.20 = (bf16[640,512]{1,0:T(8,128)(2,1)S(1)}, bf16[640,512]{1,0:T(8,128)(2,1)S(1)}, u32[]{:S(2)}, u32[]{:S(2)}) collective-permute-start(bf16[640,512]{1,0:T(8,128)(2,1)S(1)} %get-tuple-element.62), channel_id=1, source_target_pairs={{0,8},{16,24},{8,0},{24,16},{1,9},{17,25},{9,1},{25,17},{2,10},{18... | collective-permute-start | bytes 1966088 | tf_op jit(solution)/shard_map/ppermute | solution.py:215
  98.2 28.9 %collective-permute-start.24 = (bf16[640,512]{1,0:T(8,128)(2,1)S(1)}, bf16[640,512]{1,0:T(8,128)(2,1)S(1)}, u32[]{:S(2)}, u32[]{:S(2)}) collective-permute-start(bf16[640,512]{1,0:T(8,128)(2,1)S(1)} %get-tuple-element.63), channel_id=1, source_target_pairs={{8,16},{16,8},{9,17},{17,9},{10,18},{18,10},{11,19},{19,11},{12,20... | collective-permute-start | bytes 1966088 | tf_op jit(solution)/shard_map/ppermute | solution.py:215
  114.1 14.7 %collective-permute-start.17 = (bf16[512,896]{1,0:T(8,128)(2,1)S(1)}, bf16[512,896]{1,0:T(8,128)(2,1)S(1)}, u32[]{:S(2)}, u32[]{:S(2)}) collective-permute-start(bf16[512,896]{1,0:T(8,128)(2,1)S(1)} %multiply_convert_fusion), channel_id=1, source_target_pairs={{0,4},{4,0},{1,5},{5,1},{2,6},{6,2},{3,7},{7,3},{8,12},{12,8},{9,1... | collective-permute-start | bytes 2752520 | tf_op jit(solution)/shard_map/ppermute | solution.py:101
  116.3 17.1 %collective-permute-start.25 = (bf16[640,384]{1,0:T(8,128)(2,1)S(1)}, bf16[640,384]{1,0:T(8,128)(2,1)S(1)}, u32[]{:S(2)}, u32[]{:S(2)}) collective-permute-start(bf16[640,384]{1,0:T(8,128)(2,1)S(1)} %get-tuple-element.64), channel_id=1, source_target_pairs={{0,8},{16,24},{8,0},{24,16},{1,9},{17,25},{9,1},{25,17},{2,10},{18... | collective-permute-start | bytes 1474568 | tf_op jit(solution)/shard_map/ppermute | solution.py:215
  116.4 17.0 %collective-permute-start.26 = (bf16[640,384]{1,0:T(8,128)(2,1)S(1)}, bf16[640,384]{1,0:T(8,128)(2,1)S(1)}, u32[]{:S(2)}, u32[]{:S(2)}) collective-permute-start(bf16[640,384]{1,0:T(8,128)(2,1)S(1)} %get-tuple-element.65), channel_id=1, source_target_pairs={{8,16},{16,8},{9,17},{17,9},{10,18},{18,10},{11,19},{19,11},{12,20... | collective-permute-start | bytes 1474568 | tf_op jit(solution)/shard_map/ppermute | solution.py:215
  (19 other events, 108.9 us)

commit v2 on v1

v2 whole, which is shorter than its diff:
```python
import jax
import jax.numpy as jnp
from jax import lax
from jax.sharding import Mesh, PartitionSpec as P

FF = 7168
SWAP = [(0, 1), (1, 0)]
ORDER = {
    "ow": ["gw"],
    "x": ["gw"],
    "h": ["ow"],
    "d1": ["gw"],
    "sa": ["y1", "sh"],
    "d2": ["ta"],
    "sb": ["y2", "p1a"],
    "G2E": ["S1Ea"],
    "G2O": ["S1Ea"],
    "mb": ["G2E"],
    "S1Eb": ["S2Oa"],
    "S2Ea": ["S1Ea"],
    "S2Oa": ["S2Ea"],
    "G3E": ["S1Eb"],
    "S2Eb": ["G3E", "w2"],
    "S2Ob": ["S2Eb"],
    "S3Ea": ["S2Ob"],
    "S3Oa": ["S3Ea"],
    "S3Eb": ["b", "S3Oa"],
    "S3Ob": ["S3Eb"],
    "za": ["S3Ob"],
    "zb": ["out", "fa"],
    "w2": ["ta"],
    "q2": ["p1a"],
    "o2": ["p1a"],
    "q1": ["sh"],
    "o1": ["sh"],
}
EDGE = "EO"


def plane_sum(value):
    k = lax.axis_size("x") * 2
    across = [(i, k - 1 - i) for i in range(k)]
    return (
        value
        + lax.ppermute(value, "x", SWAP)
        + lax.ppermute(value, "c", SWAP)
        + lax.ppermute(value, ("x", "c"), across)
    )


def edges(n, parity, upward, downward):
    pairs = [(i, i + 1) for i in upward if i % 2 == parity]
    return pairs + [(i, i - 1) for i in downward if (i - 1) % 2 == parity]


class Graph:
    def __init__(self):
        self.rules, self.values, self.open = {}, {}, set()

    def rule(self, name, operand, work):
        self.rules[name] = (operand, work)

    def __getitem__(self, name):
        if name in self.values:
            return self.values[name]
        if name in self.open:
            raise ValueError(name)
        self.open.add(name)
        operand, work = self.rules[name]
        first = operand()
        waits = [self[other] for other in ORDER.get(name, ()) if other in self.rules]
        if waits:
            first = lax.optimization_barrier((first, waits))[0]
        self.values[name] = work(first)
        return self.values[name]


def body(d_out, gate_pre, up_pre, w_down, momentum):
    multiplier = FF ** (-0.5)
    n = lax.axis_size("z")
    z, y, x, c = (lax.axis_index(a) for a in ("z", "y", "x", "c"))
    rows = w_down.shape[0]
    height = 2 * rows
    cols = w_down.shape[1] // 2
    first = -(-cols // 256) * 128
    parts = {"a": (0, first), "b": (first, cols - first)}
    block, depth = d_out.shape
    half = n // 2 * height
    near_start = jnp.where(z < n // 2, depth - half, 0)
    starts = {"1": near_start, "2": depth - half - near_start}
    g = Graph()

    def in_order(a, b, axis):
        return jnp.where(
            y == 0, jnp.concatenate([a, b], axis=axis), jnp.concatenate([b, a], axis=axis)
        )

    def columns(a, start, width):
        return lax.dynamic_slice_in_dim(a, start, width, 1)

    def over(axis):
        return lambda value: lax.ppermute(value, axis, SWAP)

    def same(value):
        return value

    def weights(whose):
        return lambda w: columns(w, whose * cols, cols).astype(jnp.bfloat16)

    g.rule("gw", lambda: w_down, weights(1 - y))
    g.rule("ow", lambda: w_down, weights(y))
    g.rule("pw", lambda: g["gw"], over("y"))
    g.rule("sh", lambda: in_order(g["ow"], g["pw"], 0), same)
    g.rule("w2", lambda: w_down, lambda w: jnp.sum(w * w, axis=1))

    def gather_pairs(s, parity):
        return edges(n, parity, range(s - 1, n - 1), range(1, n - s + 1))

    def gather(s, parity):
        pairs = gather_pairs(s, parity)
        if not pairs:
            return
        name, got = [f"{kind}{s}{EDGE[parity]}" for kind in "GR"]
        other = f"R{s - 1}{EDGE[1 - parity]}"
        g.rule(name, (lambda: g["sh"]) if s == 1 else (lambda: g[other]), same)
        g.rule(got, lambda: g[name], lambda v: lax.ppermute(v, "z", pairs))

    for s in range(1, n):
        gather(s, 0)
        gather(s, 1)

    def hidden(operands):
        gate, up = (v.astype(jnp.float32) for v in operands)
        return (gate * jax.nn.sigmoid(gate) * up).astype(jnp.bfloat16)

    g.rule("h", lambda: (gate_pre, up_pre), hidden)

    def hidden_part(p):
        start, width = parts[p]
        g.rule("m" + p, lambda: columns(g["h"], y * cols + start, width), same)
        g.rule("s" + p, lambda: columns(g["h"], (1 - y) * cols + start, width), same)
        g.rule("t" + p, lambda: g["s" + p], over("y"))

    hidden_part("a")
    hidden_part("b")

    def arrange(operands):
        pair = jnp.concatenate(operands, axis=0)
        other = lax.ppermute(pair, "c", SWAP)
        out = jnp.zeros((4 * block, pair.shape[1]), pair.dtype)
        for source, core in ((pair, c), (other, 1 - c)):
            for k, chip in ((0, x), (1, 1 - x)):
                piece = source[k * block : (k + 1) * block]
                out = lax.dynamic_update_slice_in_dim(out, piece, (chip * 2 + core) * block, 0)
        return out

    g.rule("x", lambda: d_out, over("x"))
    g.rule("g", lambda: (d_out, g["x"]), arrange)

    def cotangents(k):
        g.rule("d" + k, lambda: columns(d_out, starts[k], half), same)
        g.rule("y" + k, lambda: g["d" + k], over("y"))
        g.rule("q" + k, lambda: g["y" + k], over("x"))
        g.rule("o" + k, lambda: (g["y" + k], g["q" + k]), arrange)

    cotangents("1")
    cotangents("2")

    contract = (((0,), (0,)), ((), ()))

    def product(k, p):
        def work(mine):
            partial = lax.dot_general(
                columns(g["g"], starts[k], half),
                mine,
                contract,
                preferred_element_type=jnp.float32,
            ) + lax.dot_general(
                g["o" + k],
                g["t" + p],
                contract,
                preferred_element_type=jnp.float32,
            )
            return (partial * multiplier).astype(jnp.bfloat16)

        g.rule("p" + k + p, lambda: g["m" + p], work)

    for k in starts:
        for p in parts:
            product(k, p)

    def chunk(p, k, s):
        k = jnp.clip(k, 0, n - 1) * height
        at = jnp.clip(k - starts["1"], 0, half - height)
        a = lax.dynamic_slice_in_dim(g["p1" + p], at, height, 0)
        if s <= n // 2:
            return a
        at = jnp.clip(k - starts["2"], 0, half - height)
        b = lax.dynamic_slice_in_dim(g["p2" + p], at, height, 0)
        return jnp.where((k >= starts["1"]) & (k < starts["1"] + half), a, b)

    def reduce(s, p, parity):
        pairs = edges(n, parity, range(0, s), range(n - s, n))
        if not pairs:
            return
        name, before = f"{s}{EDGE[parity]}{p}", f"T{s - 1}{EDGE[1 - parity]}{p}"

        def operand():
            value = chunk(p, jnp.where(z % 2 == parity, n - s + z, s - n + z), s)
            if before not in g.rules:
                return value
            got = g[before]
            return (value.astype(jnp.float32) + got.astype(jnp.float32)).astype(value.dtype)

        g.rule("S" + name, operand, same)
        g.rule("T" + name, lambda: g["S" + name], lambda v: lax.ppermute(v, "z", pairs))

    for s in range(1, n):
        for p in parts:
            reduce(s, p, 0)
            reduce(s, p, 1)

    def d_hidden_of(tokens):
        total = jnp.dot(
            columns(tokens, z * height, height), g["sh"], preferred_element_type=jnp.float32
        )
        for t in range(1, n):
            piece, place = g[f"R{t}E"], jnp.where(z % 2 == 0, z + t, z - t)
            if f"R{n - t}O" in g.rules:
                piece = jnp.where((place >= 0) & (place < n), piece, g[f"R{n - t}O"])
            total = total + jnp.dot(
                columns(tokens, place % n * height, height),
                piece,
                preferred_element_type=jnp.float32,
            )
        return (total * multiplier).astype(jnp.bfloat16)

    def other_tokens():
        a, b = g["o1"], g["o2"]
        return jnp.where(
            near_start == 0, jnp.concatenate([a, b], axis=1), jnp.concatenate([b, a], axis=1)
        )

    g.rule("b", other_tokens, d_hidden_of)
    g.rule("by", lambda: g["b"], over("y"))
    g.rule("me", lambda: g["g"], d_hidden_of)

    def gate_and_up(operands):
        gate, up = (v.astype(jnp.float32) for v in operands)
        d_hidden = in_order(g["me"], g["by"], 1).astype(jnp.float32)
        s = jax.nn.sigmoid(gate)
        d_gate = (d_hidden * up * s * (1.0 + gate * (1.0 - s))).astype(jnp.bfloat16)
        return d_gate, (d_hidden * gate * s).astype(jnp.bfloat16)

    g.rule("out", lambda: lax.optimization_barrier((gate_pre, up_pre, g["h"]))[:2], gate_and_up)

    def total(p):
        def work(even):
            whole = chunk(p, z, n).astype(jnp.float32) + even.astype(jnp.float32)
            return whole + g[f"T{n - 1}O{p}"].astype(jnp.float32)

        g.rule("z" + p, lambda: g[f"T{n - 1}E{p}"], work)

        def rows_of(whose):
            low = g["z" + p].astype(jnp.bfloat16)
            return lax.dynamic_slice_in_dim(low, whose * rows, rows, 0)

        g.rule("e" + p, lambda: rows_of(1 - y), same)
        g.rule("f" + p, lambda: g["e" + p], over("y"))
        g.rule("k" + p, lambda: rows_of(y), same)

    for p in parts:
        total(p)

    grad_square = sum(jnp.sum(g["z" + p] * g["z" + p], axis=1) for p in parts)
    keep = lax.dynamic_slice_in_dim(grad_square, y * rows, rows, 0)
    give = lax.dynamic_slice_in_dim(grad_square, (1 - y) * rows, rows, 0)
    grad_square = keep + lax.ppermute(give, "y", SWAP)
    grad_square = lax.optimization_barrier((grad_square, g["fb"]))[0]
    squares = plane_sum(jnp.stack([g["w2"], grad_square]))
    factor = jnp.minimum(1.0, 0.1 * jnp.sqrt(squares[0]) / jnp.sqrt(squares[1] + 1e-06))
    grad = in_order(
        jnp.concatenate([g["k" + p] for p in parts], 1),
        jnp.concatenate([g["f" + p] for p in parts], 1),
        1,
    ).astype(jnp.float32)
    momentum_new = 0.9 * momentum + grad * factor[:, None]
    w_new = w_down - 0.05 * momentum_new
    d_gate, d_up = g["out"]
    return (d_gate, d_up, w_new, momentum_new)


def solution(mesh):
    groups, parts = mesh.devices.shape
    fine = Mesh(mesh.devices.reshape(groups // 2, 2, parts // 2, 2), ("z", "y", "x", "c"))
    dp, tensor = ("z", "y"), ("x", "c")
    placed = P(dp, tensor)
    return jax.shard_map(
        body,
        mesh=fine,
        in_specs=(P(dp + tensor, None), placed, placed, placed, placed),
        out_specs=(placed,) * 4,
        check_vma=False,
    )
```

time: 151 us -> 153 us (1.013)
  waiting for transfers between devices: 49.4 us -> 52.2 us
    ppermute x1, waiting for transfers between devices: 1.45 us -> 4.11 us  [body(): grad_square = keep + lax.ppermute(give, 'y', SWAP)]
where the time goes in v2:
time: 153 us; the launch traced here: 152 us
  waiting for transfers between devices  52.2 us (34%)
  starting transfers between devices  50.8 us (33%)
  other arithmetic  17.8 us (12%)
  local copies, waits for them, and re-layouts  15.4 us (10%)
  matrix products  15 us (10%)
    ppermute x10, starting transfers between devices, reduce(): lax.ppermute(v, 'z', pairs)  22.6 us
    ppermute x10, waiting for transfers between devices, reduce(): lax.ppermute(v, 'z', pairs)  19.4 us
    ppermute x11, starting transfers between devices, over(): return lambda value: lax.ppermute(value, axis, SWAP)  16.5 us
    ppermute x5, waiting for transfers between devices, gather(): g.rule(got, lambda: g[name], lambda v: lax.ppermute(v, 'z', pairs))  14.8 us
    ppermute x11, waiting for transfers between devices, over(): return lambda value: lax.ppermute(value, axis, SWAP)  11 us
    ppermute x5, starting transfers between devices, gather(): g.rule(got, lambda: g[name], lambda v: lax.ppermute(v, 'z', pairs))  8.84 us
    dot_general x6, matrix products, d_hidden_of(): jnp.dot(columns(tokens, place % n * height, height), piece, preferred_ele...  6.04 us
    dynamic_slice x3, local copies, waits for them, and re-layouts, columns(): return lax.dynamic_slice_in_dim(a, start, width, 1)  5.11 us
  transfers between devices with their start and end apart: 33, of which 13 were waited for; matrix products, arithmetic and copies ran while one was open for 27% of the time, Pallas kernels for 0%

profile of v2, /device:TPU:0, one launch (start us, length us, event | category | flops | bytes accessed | tf_op | source)
XLA Modules:
  0.0 152.4 jit_solution(3311046837316339901)
XLA Ops:
  0.7 2.3 %dynamic-slice_convert_fusion.1 = bf16[320,896]{1,0:T(8,128)(2,1)} fusion(f32[320,1792]{1,0:T(8,128)} %param.8, s32[]{:T(128)S(6)} %select_n.261), kind=kLoop, calls=%fused_computation.52 | loop fusion | bytes 1146884 | tf_op jit(solution)/shard_map/convert_element_type | solution.py:108
  2.9 3.0 %collective-permute-start.2 = (bf16[320,896]{1,0:T(8,128)(2,1)}, bf16[320,896]{1,0:T(8,128)(2,1)}, u32[]{:S(2)}, u32[]{:S(2)}) collective-permute-start(bf16[320,896]{1,0:T(8,128)(2,1)} %dynamic-slice_convert_fusion.1), channel_id=1, source_target_pairs={{0,4},{4,0},{1,5},{5,1},{2,6},{6,2},{3,7},{7,3},{8,12},{12,8},{9,1... | collective-permute-start | bytes 1720328 | tf_op jit(solution)/shard_map/ppermute | solution.py:102
  7.4 1.9 %constant_dynamic-slice_fusion.7 = (bf16[128,1280]{1,0:T(8,128)(2,1)}, bf16[128,1280]{1,0:T(8,128)(2,1)}) fusion(bf16[128,2560]{1,0:T(8,128)(2,1)} %param.5, s32[]{:T(128)S(6)} %select_n.285, s32[]{:T(128)S(6)} %select_n.277), kind=kLoop, calls=%fused_computation.106 | loop fusion | bytes 1310728 | tf_op jit(solution)/shard_map/dynamic_slice | solution.py:99
  9.8 2.1 %dynamic-slice_convert_fusion = bf16[320,896]{1,0:T(8,128)(2,1)} fusion(f32[320,1792]{1,0:T(8,128)} %param.8, s32[]{:T(128)S(6)} %select_n.267), kind=kLoop, calls=%fused_computation.51 | loop fusion | bytes 1146884 | tf_op jit(solution)/shard_map/convert_element_type | solution.py:108
  12.0 3.8 %fusion.13 = bf16[512,1792]{1,0:T(8,128)(2,1)} fusion(bf16[512,1792]{1,0:T(8,128)(2,1)} %param.7, bf16[512,1792]{1,0:T(8,128)(2,1)S(1)} %copy-done.2), kind=kLoop, calls=%fused_computation.19 | loop fusion | flops 7340032 | bytes 5505024 | tf_op jit(solution)/shard_map/convert_element_type | solution.py:134
  16.9 1.9 %constant_dynamic-slice_fusion.11 = bf16[512,512]{1,0:T(8,128)(2,1)} fusion(bf16[512,1792]{1,0:T(8,128)(2,1)} %fusion.13, s32[]{:T(128)S(6)} %select_n.261), kind=kLoop, calls=%fused_computation.111 | loop fusion | bytes 1048580 | tf_op jit(solution)/shard_map/dynamic_slice | solution.py:99
  22.4 4.8 %collective-permute-start.3 = (bf16[640,896]{1,0:T(8,128)(2,1)S(1)}, bf16[640,896]{1,0:T(8,128)(2,1)S(1)}, u32[]{:S(2)}, u32[]{:S(2)}) collective-permute-start(bf16[640,896]{1,0:T(8,128)(2,1)S(1)} %maximum_select_fusion.2), channel_id=1, source_target_pairs={{0,8},{16,24},{8,0},{24,16},{1,9},{17,25},{9,1},{25,17},{2,10},{18... | collective-permute-start | bytes 3440648 | tf_op jit(solution)/shard_map/ppermute | solution.py:126
  32.7 2.6 %collective-permute-done.6 = bf16[128,1280]{1,0:T(8,128)(2,1)S(1)} collective-permute-done((bf16[128,1280]{1,0:T(8,128)(2,1)}, bf16[128,1280]{1,0:T(8,128)(2,1)S(1)}, u32[]{:S(2)}, u32[]{:S(2)}) %collective-permute-start.6) | collective-permute-done | bytes 327712 | tf_op jit(solution)/shard_map/ppermute | solution.py:102
  37.5 2.9 %collective-permute-done.8 = bf16[512,512]{1,0:T(8,128)(2,1)S(1)} collective-permute-done((bf16[512,512]{1,0:T(8,128)(2,1)S(1)}, bf16[512,512]{1,0:T(8,128)(2,1)S(1)}, u32[]{:S(2)}, u32[]{:S(2)}) %collective-permute-start.8) | collective-permute-done | bytes 524320 | tf_op jit(solution)/shard_map/ppermute | solution.py:102
  45.9 3.5 %collective-permute-start.13 = (bf16[640,512]{1,0:T(8,128)(2,1)S(1)}, bf16[640,512]{1,0:T(8,128)(2,1)S(1)}, u32[]{:S(2)}, u32[]{:S(2)}) collective-permute-start(bf16[640,512]{1,0:T(8,128)(2,1)S(1)} %get-tuple-element.85), channel_id=1, source_target_pairs={{0,8},{24,16},{1,9},{25,17},{2,10},{26,18},{3,11},{27,19},{4,12},{... | collective-permute-start | bytes 1966088 | tf_op jit(solution)/shard_map/ppermute | solution.py:216
  56.2 1.6 %collective-permute-done.15 = bf16[128,1280]{1,0:T(8,128)(2,1)S(1)} collective-permute-done((bf16[128,1280]{1,0:T(8,128)(2,1)S(1)}, bf16[128,1280]{1,0:T(8,128)(2,1)S(1)}, u32[]{:S(2)}, u32[]{:S(2)}) %collective-permute-start.15) | collective-permute-done | bytes 327712 | tf_op jit(solution)/shard_map/ppermute | solution.py:102
  57.9 4.6 %collective-permute-start.23 = (bf16[640,512]{1,0:T(8,128)(2,1)S(1)}, bf16[640,512]{1,0:T(8,128)(2,1)S(1)}, u32[]{:S(2)}, u32[]{:S(2)}) collective-permute-start(bf16[640,512]{1,0:T(8,128)(2,1)S(1)} %get-tuple-element.51), channel_id=1, source_target_pairs={{0,8},{24,16},{1,9},{25,17},{2,10},{26,18},{3,11},{27,19},{4,12},{... | collective-permute-start | bytes 1966088 | tf_op jit(solution)/shard_map/ppermute | solution.py:216
  64.9 2.1 %collective-permute-done.13 = bf16[640,512]{1,0:T(8,128)(2,1)S(1)} collective-permute-done((bf16[640,512]{1,0:T(8,128)(2,1)S(1)}, bf16[640,512]{1,0:T(8,128)(2,1)S(1)}, u32[]{:S(2)}, u32[]{:S(2)}) %collective-permute-start.13) | collective-permute-done | bytes 655392 | tf_op jit(solution)/shard_map/ppermute | solution.py:216
  68.0 5.8 %collective-permute-start.19 = (bf16[640,384]{1,0:T(8,128)(2,1)S(1)}, bf16[640,384]{1,0:T(8,128)(2,1)S(1)}, u32[]{:S(2)}, u32[]{:S(2)}) collective-permute-start(bf16[640,384]{1,0:T(8,128)(2,1)S(1)} %get-tuple-element.53), channel_id=1, source_target_pairs={{0,8},{24,16},{1,9},{25,17},{2,10},{26,18},{3,11},{27,19},{4,12},{... | collective-permute-start | bytes 1474568 | tf_op jit(solution)/shard_map/ppermute | solution.py:216
  81.3 7.5 %collective-permute-done.19 = bf16[640,384]{1,0:T(8,128)(2,1)S(1)} collective-permute-done((bf16[640,384]{1,0:T(8,128)(2,1)S(1)}, bf16[640,384]{1,0:T(8,128)(2,1)S(1)}, u32[]{:S(2)}, u32[]{:S(2)}) %collective-permute-start.19) | collective-permute-done | bytes 491552 | tf_op jit(solution)/shard_map/ppermute | solution.py:216
  89.1 4.4 %collective-permute-start.21 = (bf16[640,384]{1,0:T(8,128)(2,1)S(1)}, bf16[640,384]{1,0:T(8,128)(2,1)S(1)}, u32[]{:S(2)}, u32[]{:S(2)}) collective-permute-start(bf16[640,384]{1,0:T(8,128)(2,1)S(1)} %get-tuple-element.61), channel_id=1, source_target_pairs={{0,8},{24,16},{1,9},{25,17},{2,10},{26,18},{3,11},{27,19},{4,12},{... | collective-permute-start | bytes 1474568 | tf_op jit(solution)/shard_map/ppermute | solution.py:216
  98.9 14.1 %collective-permute-done.14 = bf16[640,896]{1,0:T(8,128)(2,1)S(1)} collective-permute-done((bf16[640,896]{1,0:T(8,128)(2,1)S(1)}, bf16[640,896]{1,0:T(8,128)(2,1)S(1)}, u32[]{:S(2)}, u32[]{:S(2)}) %collective-permute-start.14) | collective-permute-done | bytes 1146912 | tf_op jit(solution)/shard_map/ppermute | solution.py:126
  117.3 9.7 %collective-permute-done.20 = bf16[640,512]{1,0:T(8,128)(2,1)S(1)} collective-permute-done((bf16[640,512]{1,0:T(8,128)(2,1)S(1)}, bf16[640,512]{1,0:T(8,128)(2,1)S(1)}, u32[]{:S(2)}, u32[]{:S(2)}) %collective-permute-start.20) | collective-permute-done | bytes 655392 | tf_op jit(solution)/shard_map/ppermute | solution.py:216
  131.7 3.4 %fusion.12 = (bf16[512,1792]{1,0:T(8,128)(2,1)}, bf16[512,1792]{1,0:T(8,128)(2,1)}) fusion(bf16[512,1792]{1,0:T(8,128)(2,1)S(1)} %copy-done.3, bf16[512,896]{1,0:T(8,128)(2,1)S(1)} %multiply_convert_fusion.1, bf16[512,896]{1,0:T(8,128)(2,1)S(1)} %collective-permute-done.17, pred[]{:T(512)S(6)} %eq.51, bf16[512,1792]{1,0:T(8,128)(2,1)S(1)} %copy-done.4), kind=kLoop, calls=%fused_computation.18 | loop fusion | flops 22937600 | bytes 9175041 | tf_op jit(solution)/shard_map/convert_element_type | solution.py:253
  135.2 2.6 %collective-permute-done.26 = bf16[320,512]{1,0:T(8,128)(2,1)S(1)} collective-permute-done((bf16[320,512]{1,0:T(8,128)(2,1)S(1)}, bf16[320,512]{1,0:T(8,128)(2,1)S(1)}, u32[]{:S(2)}, u32[]{:S(2)}) %collective-permute-start.26) | collective-permute-done | bytes 327712 | tf_op jit(solution)/shard_map/ppermute | solution.py:102
  138.3 1.6 %collective-permute-start.28 = (bf16[320,384]{1,0:T(8,128)(2,1)S(1)}, bf16[320,384]{1,0:T(8,128)(2,1)S(1)}, u32[]{:S(2)}, u32[]{:S(2)}) collective-permute-start(bf16[320,384]{1,0:T(8,128)(2,1)S(1)} %get-tuple-element.93), channel_id=1, source_target_pairs={{0,4},{4,0},{1,5},{5,1},{2,6},{6,2},{3,7},{7,3},{8,12},{12,8},{9,1... | collective-permute-start | bytes 737288 | tf_op jit(solution)/shard_map/ppermute | solution.py:102
  140.5 4.1 %collective-permute-done.29 = f32[320]{0:T(512)S(1)} collective-permute-done((f32[320]{0:T(512)S(1)}, f32[320]{0:T(512)S(1)}, u32[]{:S(2)}, u32[]{:S(2)}) %collective-permute-start.29) | collective-permute-done | bytes 1312 | tf_op jit(solution)/shard_map/ppermute | solution.py:278
  147.8 2.0 %collective-permute-done.30 = f32[2,320]{1,0:T(2,128)S(1)} collective-permute-done((f32[2,320]{1,0:T(2,128)S(1)}, f32[2,320]{1,0:T(2,128)S(1)}, u32[]{:S(2)}, u32[]{:S(2)}) %collective-permute-start.30) | collective-permute-done | bytes 2592 | tf_op jit(solution)/shard_map/ppermute | solution.py:45
  149.9 2.6 %multiply_subtract_fusion = (f32[320,1792]{1,0:T(8,128)}, f32[320,1792]{1,0:T(8,128)}) fusion(f32[320,1792]{1,0:T(8,128)S(1)} %copy-done, f32[320]{0:T(512)S(1)} %minimum_reduce_fusion, bf16[320,384]{1,0:T(8,128)(2,1)S(1)} %get-tuple-element.92, bf16[320,512]{1,0:T(8,128)(2,1)S(1)} %get-tuple-element.88, bf16[320,384]{1,0:T(8,128)(2,1)S(1)} %collective-permute-done.28, ...), kind=kLoop, calls=%fused_computation.33 | loop fusion | flops 13189120 | bytes 10323201 | tf_op jit(solution)/shard_map/sub | solution.py:288
  (125 shorter events, 56.1 us)
Async XLA Ops:
  2.9 17.2 %collective-permute-start.2 = (bf16[320,896]{1,0:T(8,128)(2,1)}, bf16[320,896]{1,0:T(8,128)(2,1)}, u32[]{:S(2)}, u32[]{:S(2)}) collective-permute-start(bf16[320,896]{1,0:T(8,128)(2,1)} %dynamic-slice_convert_fusion.1), channel_id=1, source_target_pairs={{0,4},{4,0},{1,5},{5,1},{2,6},{6,2},{3,7},{7,3},{8,12},{12,8},{9,1... | collective-permute-start | bytes 1720328 | tf_op jit(solution)/shard_map/ppermute | solution.py:102
  5.9 24.4 %collective-permute-start = (bf16[128,2560]{1,0:T(8,128)(2,1)}, bf16[128,2560]{1,0:T(8,128)(2,1)}, u32[]{:S(2)}, u32[]{:S(2)}) collective-permute-start(bf16[128,2560]{1,0:T(8,128)(2,1)} %param.5), channel_id=1, source_target_pairs={{0,2},{2,0},{1,3},{3,1},{4,6},{6,4},{5,7},{7,5},{8,10},{10,8},{9,1... | collective-permute-start | bytes 1966088 | tf_op jit(solution)/shard_map/ppermute | solution.py:102
  9.3 17.9 %collective-permute-start.5 = (bf16[128,1280]{1,0:T(8,128)(2,1)}, bf16[128,1280]{1,0:T(8,128)(2,1)}, u32[]{:S(2)}, u32[]{:S(2)}) collective-permute-start(bf16[128,1280]{1,0:T(8,128)(2,1)} %get-tuple-element.41), channel_id=1, source_target_pairs={{0,4},{4,0},{1,5},{5,1},{2,6},{6,2},{3,7},{7,3},{8,12},{12,8},{9,1... | collective-permute-start | bytes 983048 | tf_op jit(solution)/shard_map/ppermute | solution.py:102
  21.7 27.7 %collective-permute-start.4 = (bf16[640,896]{1,0:T(8,128)(2,1)S(1)}, bf16[640,896]{1,0:T(8,128)(2,1)S(1)}, u32[]{:S(2)}, u32[]{:S(2)}) collective-permute-start(bf16[640,896]{1,0:T(8,128)(2,1)S(1)} %maximum_select_fusion.2), channel_id=1, source_target_pairs={{8,16},{16,8},{9,17},{17,9},{10,18},{18,10},{11,19},{19,11},{12,20... | collective-permute-start | bytes 3440648 | tf_op jit(solution)/shard_map/ppermute | solution.py:126
  22.4 30.5 %collective-permute-start.3 = (bf16[640,896]{1,0:T(8,128)(2,1)S(1)}, bf16[640,896]{1,0:T(8,128)(2,1)S(1)}, u32[]{:S(2)}, u32[]{:S(2)}) collective-permute-start(bf16[640,896]{1,0:T(8,128)(2,1)S(1)} %maximum_select_fusion.2), channel_id=1, source_target_pairs={{0,8},{16,24},{8,0},{24,16},{1,9},{17,25},{9,1},{25,17},{2,10},{18... | collective-permute-start | bytes 3440648 | tf_op jit(solution)/shard_map/ppermute | solution.py:126
  28.7 11.7 %collective-permute-start.8 = (bf16[512,512]{1,0:T(8,128)(2,1)S(1)}, bf16[512,512]{1,0:T(8,128)(2,1)S(1)}, u32[]{:S(2)}, u32[]{:S(2)}) collective-permute-start(bf16[512,512]{1,0:T(8,128)(2,1)S(1)} %copy-done.8), channel_id=1, source_target_pairs={{0,4},{4,0},{1,5},{5,1},{2,6},{6,2},{3,7},{7,3},{8,12},{12,8},{9,1... | collective-permute-start | bytes 1572872 | tf_op jit(solution)/shard_map/ppermute | solution.py:102
  31.4 11.7 %collective-permute-start.1 = (bf16[256,2560]{1,0:T(8,128)(2,1)S(1)}, bf16[256,2560]{1,0:T(8,128)(2,1)S(1)}, u32[]{:S(2)}, u32[]{:S(2)}) collective-permute-start(bf16[256,2560]{1,0:T(8,128)(2,1)S(1)} %pad_maximum_fusion), channel_id=1, source_target_pairs={{0,1},{1,0},{2,3},{3,2},{4,5},{5,4},{6,7},{7,6},{8,9},{9,8},{10,11... | collective-permute-start | bytes 3932168 | tf_op jit(solution)/shard_map/ppermute | solution.py:149
  40.4 10.3 %collective-permute-start.11 = (bf16[128,1280]{1,0:T(8,128)(2,1)S(1)}, bf16[128,1280]{1,0:T(8,128)(2,1)S(1)}, u32[]{:S(2)}, u32[]{:S(2)}) collective-permute-start(bf16[128,1280]{1,0:T(8,128)(2,1)S(1)} %copy-done.9), channel_id=1, source_target_pairs={{0,4},{4,0},{1,5},{5,1},{2,6},{6,2},{3,7},{7,3},{8,12},{12,8},{9,1... | collective-permute-start | bytes 983048 | tf_op jit(solution)/shard_map/ppermute | solution.py:102
  45.9 21.1 %collective-permute-start.13 = (bf16[640,512]{1,0:T(8,128)(2,1)S(1)}, bf16[640,512]{1,0:T(8,128)(2,1)S(1)}, u32[]{:S(2)}, u32[]{:S(2)}) collective-permute-start(bf16[640,512]{1,0:T(8,128)(2,1)S(1)} %get-tuple-element.85), channel_id=1, source_target_pairs={{0,8},{24,16},{1,9},{25,17},{2,10},{26,18},{3,11},{27,19},{4,12},{... | collective-permute-start | bytes 1966088 | tf_op jit(solution)/shard_map/ppermute | solution.py:216
  49.4 44.1 %collective-permute-start.9 = (bf16[640,896]{1,0:T(8,128)(2,1)S(1)}, bf16[640,896]{1,0:T(8,128)(2,1)S(1)}, u32[]{:S(2)}, u32[]{:S(2)}) collective-permute-start(bf16[640,896]{1,0:T(8,128)(2,1)S(1)} %collective-permute-done.4), channel_id=1, source_target_pairs={{16,24},{8,0},{17,25},{9,1},{18,26},{10,2},{19,27},{11,3},{20,28},... | collective-permute-start | bytes 3440648 | tf_op jit(solution)/shard_map/ppermute | solution.py:126
  53.0 27.0 %collective-permute-start.10 = (bf16[640,896]{1,0:T(8,128)(2,1)S(1)}, bf16[640,896]{1,0:T(8,128)(2,1)S(1)}, u32[]{:S(2)}, u32[]{:S(2)}) collective-permute-start(bf16[640,896]{1,0:T(8,128)(2,1)S(1)} %collective-permute-done.3), channel_id=1, source_target_pairs={{8,16},{16,8},{9,17},{17,9},{10,18},{18,10},{11,19},{19,11},{12,20... | collective-permute-start | bytes 3440648 | tf_op jit(solution)/shard_map/ppermute | solution.py:126
  53.7 9.0 %collective-permute-start.12 = (bf16[512,384]{1,0:T(8,128)(2,1)S(1)}, bf16[512,384]{1,0:T(8,128)(2,1)S(1)}, u32[]{:S(2)}, u32[]{:S(2)}) collective-permute-start(bf16[512,384]{1,0:T(8,128)(2,1)S(1)} %get-tuple-element.50), channel_id=1, source_target_pairs={{0,4},{4,0},{1,5},{5,1},{2,6},{6,2},{3,7},{7,3},{8,12},{12,8},{9,1... | collective-permute-start | bytes 1179656 | tf_op jit(solution)/shard_map/ppermute | solution.py:102
  57.9 38.3 %collective-permute-start.23 = (bf16[640,512]{1,0:T(8,128)(2,1)S(1)}, bf16[640,512]{1,0:T(8,128)(2,1)S(1)}, u32[]{:S(2)}, u32[]{:S(2)}) collective-permute-start(bf16[640,512]{1,0:T(8,128)(2,1)S(1)} %get-tuple-element.51), channel_id=1, source_target_pairs={{0,8},{24,16},{1,9},{25,17},{2,10},{26,18},{3,11},{27,19},{4,12},{... | collective-permute-start | bytes 1966088 | tf_op jit(solution)/shard_map/ppermute | solution.py:216
  67.3 28.9 %collective-permute-start.18 = (bf16[640,512]{1,0:T(8,128)(2,1)S(1)}, bf16[640,512]{1,0:T(8,128)(2,1)S(1)}, u32[]{:S(2)}, u32[]{:S(2)}) collective-permute-start(bf16[640,512]{1,0:T(8,128)(2,1)S(1)} %add_convert_fusion.2), channel_id=1, source_target_pairs={{8,16},{16,8},{9,17},{17,9},{10,18},{18,10},{11,19},{19,11},{12,20... | collective-permute-start | bytes 1966088 | tf_op jit(solution)/shard_map/ppermute | solution.py:216
  68.0 20.9 %collective-permute-start.19 = (bf16[640,384]{1,0:T(8,128)(2,1)S(1)}, bf16[640,384]{1,0:T(8,128)(2,1)S(1)}, u32[]{:S(2)}, u32[]{:S(2)}) collective-permute-start(bf16[640,384]{1,0:T(8,128)(2,1)S(1)} %get-tuple-element.53), channel_id=1, source_target_pairs={{0,8},{24,16},{1,9},{25,17},{2,10},{26,18},{3,11},{27,19},{4,12},{... | collective-permute-start | bytes 1474568 | tf_op jit(solution)/shard_map/ppermute | solution.py:216
  80.0 33.0 %collective-permute-start.14 = (bf16[640,896]{1,0:T(8,128)(2,1)S(1)}, bf16[640,896]{1,0:T(8,128)(2,1)S(1)}, u32[]{:S(2)}, u32[]{:S(2)}) collective-permute-start(bf16[640,896]{1,0:T(8,128)(2,1)S(1)} %collective-permute-done.10), channel_id=1, source_target_pairs={{16,24},{8,0},{17,25},{9,1},{18,26},{10,2},{19,27},{11,3},{20,28},... | collective-permute-start | bytes 3440648 | tf_op jit(solution)/shard_map/ppermute | solution.py:126
  89.1 26.6 %collective-permute-start.21 = (bf16[640,384]{1,0:T(8,128)(2,1)S(1)}, bf16[640,384]{1,0:T(8,128)(2,1)S(1)}, u32[]{:S(2)}, u32[]{:S(2)}) collective-permute-start(bf16[640,384]{1,0:T(8,128)(2,1)S(1)} %get-tuple-element.61), channel_id=1, source_target_pairs={{0,8},{24,16},{1,9},{25,17},{2,10},{26,18},{3,11},{27,19},{4,12},{... | collective-permute-start | bytes 1474568 | tf_op jit(solution)/shard_map/ppermute | solution.py:216
  93.5 22.2 %collective-permute-start.22 = (bf16[640,384]{1,0:T(8,128)(2,1)S(1)}, bf16[640,384]{1,0:T(8,128)(2,1)S(1)}, u32[]{:S(2)}, u32[]{:S(2)}) collective-permute-start(bf16[640,384]{1,0:T(8,128)(2,1)S(1)} %add_convert_fusion.5), channel_id=1, source_target_pairs={{8,16},{16,8},{9,17},{17,9},{10,18},{18,10},{11,19},{19,11},{12,20... | collective-permute-start | bytes 1474568 | tf_op jit(solution)/shard_map/ppermute | solution.py:216
  97.1 29.9 %collective-permute-start.20 = (bf16[640,512]{1,0:T(8,128)(2,1)S(1)}, bf16[640,512]{1,0:T(8,128)(2,1)S(1)}, u32[]{:S(2)}, u32[]{:S(2)}) collective-permute-start(bf16[640,512]{1,0:T(8,128)(2,1)S(1)} %get-tuple-element.63), channel_id=1, source_target_pairs={{0,8},{16,24},{8,0},{24,16},{1,9},{17,25},{9,1},{25,17},{2,10},{18... | collective-permute-start | bytes 1966088 | tf_op jit(solution)/shard_map/ppermute | solution.py:216
  98.2 28.9 %collective-permute-start.24 = (bf16[640,512]{1,0:T(8,128)(2,1)S(1)}, bf16[640,512]{1,0:T(8,128)(2,1)S(1)}, u32[]{:S(2)}, u32[]{:S(2)}) collective-permute-start(bf16[640,512]{1,0:T(8,128)(2,1)S(1)} %get-tuple-element.64), channel_id=1, source_target_pairs={{8,16},{16,8},{9,17},{17,9},{10,18},{18,10},{11,19},{19,11},{12,20... | collective-permute-start | bytes 1966088 | tf_op jit(solution)/shard_map/ppermute | solution.py:216
  114.1 17.6 %collective-permute-start.17 = (bf16[512,896]{1,0:T(8,128)(2,1)S(1)}, bf16[512,896]{1,0:T(8,128)(2,1)S(1)}, u32[]{:S(2)}, u32[]{:S(2)}) collective-permute-start(bf16[512,896]{1,0:T(8,128)(2,1)S(1)} %multiply_convert_fusion), channel_id=1, source_target_pairs={{0,4},{4,0},{1,5},{5,1},{2,6},{6,2},{3,7},{7,3},{8,12},{12,8},{9,1... | collective-permute-start | bytes 2752520 | tf_op jit(solution)/shard_map/ppermute | solution.py:102
  116.3 21.4 %collective-permute-start.25 = (bf16[640,384]{1,0:T(8,128)(2,1)S(1)}, bf16[640,384]{1,0:T(8,128)(2,1)S(1)}, u32[]{:S(2)}, u32[]{:S(2)}) collective-permute-start(bf16[640,384]{1,0:T(8,128)(2,1)S(1)} %get-tuple-element.65), channel_id=1, source_target_pairs={{0,8},{16,24},{8,0},{24,16},{1,9},{17,25},{9,1},{25,17},{2,10},{18... | collective-permute-start | bytes 1474568 | tf_op jit(solution)/shard_map/ppermute | solution.py:216
  116.4 21.3 %collective-permute-start.27 = (bf16[640,384]{1,0:T(8,128)(2,1)S(1)}, bf16[640,384]{1,0:T(8,128)(2,1)S(1)}, u32[]{:S(2)}, u32[]{:S(2)}) collective-permute-start(bf16[640,384]{1,0:T(8,128)(2,1)S(1)} %get-tuple-element.66), channel_id=1, source_target_pairs={{8,16},{16,8},{9,17},{17,9},{10,18},{18,10},{11,19},{19,11},{12,20... | collective-permute-start | bytes 1474568 | tf_op jit(solution)/shard_map/ppermute | solution.py:216
  127.8 10.0 %collective-permute-start.26 = (bf16[320,512]{1,0:T(8,128)(2,1)S(1)}, bf16[320,512]{1,0:T(8,128)(2,1)S(1)}, u32[]{:S(2)}, u32[]{:S(2)}) collective-permute-start(bf16[320,512]{1,0:T(8,128)(2,1)S(1)} %get-tuple-element.89), channel_id=1, source_target_pairs={{0,4},{4,0},{1,5},{5,1},{2,6},{6,2},{3,7},{7,3},{8,12},{12,8},{9,1... | collective-permute-start | bytes 983048 | tf_op jit(solution)/shard_map/ppermute | solution.py:102
  (19 other events, 111.8 us)

commit v3 on v2

--- a/solution.py
+++ b/solution.py
@@ -12,27 +12,27 @@
     "d1": ["gw"],
     "sa": ["y1", "sh"],
     "d2": ["ta"],
-    "sb": ["y2", "p1a"],
-    "G2E": ["S1Ea"],
+    "sb": ["y2", "S1Ea"],
+    "G2E": ["S1Ea", "G2O"],
     "G2O": ["S1Ea"],
     "mb": ["G2E"],
     "S1Eb": ["S2Oa"],
     "S2Ea": ["S1Ea"],
     "S2Oa": ["S2Ea"],
     "G3E": ["S1Eb"],
-    "S2Eb": ["G3E", "w2"],
-    "S2Ob": ["S2Eb"],
-    "S3Ea": ["S2Ob"],
-    "S3Oa": ["S3Ea"],
-    "S3Eb": ["b", "S3Oa"],
+    "S2Ob": ["S3Ea", "T3Oa"],
+    "S3Ea": ["S3Oa", "w2"],
+    "S3Oa": ["G3E"],
+    "S3Eb": ["b", "S2Ob"],
     "S3Ob": ["S3Eb"],
     "za": ["S3Ob"],
-    "zb": ["out", "fa"],
+    "zb": ["by"],
     "w2": ["ta"],
-    "q2": ["p1a"],
-    "o2": ["p1a"],
+    "q2": ["S1Ea"],
+    "o2": ["S1Ea"],
     "q1": ["sh"],
     "o1": ["sh"],
+    "G1O": ["G1E"],
 }
 EDGE = "EO"
 
@@ -215,9 +215,28 @@
         g.rule("S" + name, operand, same)
         g.rule("T" + name, lambda: g["S" + name], lambda v: lax.ppermute(v, "z", pairs))
 
+    def first_two(p):
+        pairs = edges(n, 0, range(0, 1), range(n - 1, n))
+        at = jnp.where(z % 2 == 0, (n - 2) * height, 0) - starts["1"]
+
+        def operand():
+            at_most = jnp.clip(at, 0, half - 2 * height)
+            return lax.dynamic_slice_in_dim(g["p1" + p], at_most, 2 * height, 0)
+
+        g.rule("S1E" + p, operand, same)
+        g.rule("U" + p, lambda: g["S1E" + p], lambda v: lax.ppermute(v, "z", pairs))
+        for s, start in ((1, z % 2 * height), (2, (1 - z % 2) * height)):
+            g.rule(f"T{s}E{p}", part_of("U" + p, start), same)
+
+    def part_of(name, start):
+        return lambda: lax.dynamic_slice_in_dim(g[name], start, height, 0)
+
     for s in range(1, n):
         for p in parts:
-            reduce(s, p, 0)
+            if p == "a" or s > 2:
+                reduce(s, p, 0)
+            elif s == 1:
+                first_two(p)
             reduce(s, p, 1)
 
     def d_hidden_of(tokens):
@@ -272,11 +291,11 @@
     for p in parts:
         total(p)
 
-    grad_square = sum(jnp.sum(g["z" + p] * g["z" + p], axis=1) for p in parts)
-    keep = lax.dynamic_slice_in_dim(grad_square, y * rows, rows, 0)
-    give = lax.dynamic_slice_in_dim(grad_square, (1 - y) * rows, rows, 0)
-    grad_square = keep + lax.ppermute(give, "y", SWAP)
-    grad_square = lax.optimization_barrier((grad_square, g["fb"]))[0]
+    def square_sum(name):
+        value = g[name].astype(jnp.float32)
+        return jnp.sum(value * value, axis=1)
+
+    grad_square = sum(square_sum(kind + p) for p in parts for kind in "kf")
     squares = plane_sum(jnp.stack([g["w2"], grad_square]))
     factor = jnp.minimum(1.0, 0.1 * jnp.sqrt(squares[0]) / jnp.sqrt(squares[1] + 1e-06))
     grad = in_order(

time: 153 us -> 151 us (0.987)
  waiting for transfers between devices: 52.2 us -> 36.1 us
  starting transfers between devices: 50.8 us -> 64.9 us
    ppermute x10 -> x8, waiting for transfers between devices: 19.4 us -> 7 us  [reduce(): lax.ppermute(v, 'z', pairs)]
    ppermute x10 -> x8, starting transfers between devices: 22.6 us -> 33.6 us  [reduce(): lax.ppermute(v, 'z', pairs)]
    ppermute x11, waiting for transfers between devices: 11 us -> 19.8 us  [over(): return lambda value: lax.ppermute(value, axis, SWAP)]
    ppermute x5, waiting for transfers between devices: 14.8 us -> 9.29 us  [gather(): g.rule(got, lambda: g[name], lambda v: lax.ppermute(v, 'z', pairs))]
    ppermute x1, starting transfers between devices: 0.48 us -> 5.75 us  [first_two(): g.rule('U' + p, lambda: g['S1E' + p], lambda v: lax.ppermute(v, 'z', pairs))]
    ppermute x1, waiting for transfers between devices: 4.11 us -> 0.01 us  [first_two(): g.rule('U' + p, lambda: g['S1E' + p], lambda v: lax.ppermute(v, 'z', pairs))]
    ppermute x5, starting transfers between devices: 8.84 us -> 6.06 us  [gather(): g.rule(got, lambda: g[name], lambda v: lax.ppermute(v, 'z', pairs))]
    ppermute x1, waiting for transfers between devices: 2 us -> 0.01 us  [plane_sum(): lax.ppermute(value, 'x', SWAP)]
  transfers between devices with their start and end apart: 33 -> 31, of which waited for: 13 -> 10; matrix products, arithmetic and copies ran while one was open for 27% -> 27% of each run, Pallas kernels for 0% -> 0%
where the time goes in v3:
time: 151 us; the launch traced here: 150 us
  starting transfers between devices  64.9 us (43%)
  waiting for transfers between devices  36.1 us (24%)
  other arithmetic  18.1 us (12%)
  local copies, waits for them, and re-layouts  15.1 us (10%)
  matrix products  15 us (10%)
    ppermute x8, starting transfers between devices, reduce(): lax.ppermute(v, 'z', pairs)  33.6 us
    ppermute x11, waiting for transfers between devices, over(): return lambda value: lax.ppermute(value, axis, SWAP)  19.8 us
    ppermute x11, starting transfers between devices, over(): return lambda value: lax.ppermute(value, axis, SWAP)  17.1 us
    ppermute x5, waiting for transfers between devices, gather(): g.rule(got, lambda: g[name], lambda v: lax.ppermute(v, 'z', pairs))  9.29 us
    ppermute x8, waiting for transfers between devices, reduce(): lax.ppermute(v, 'z', pairs)  7 us
    ppermute x5, starting transfers between devices, gather(): g.rule(got, lambda: g[name], lambda v: lax.ppermute(v, 'z', pairs))  6.06 us
    dot_general x6, matrix products, d_hidden_of(): jnp.dot(columns(tokens, place % n * height, height), piece, preferred_ele...  6.05 us
    ppermute x1, starting transfers between devices, first_two(): g.rule('U' + p, lambda: g['S1E' + p], lambda v: lax.ppermute(v, 'z', pairs))  5.75 us
  transfers between devices with their start and end apart: 31, of which 10 were waited for; matrix products, arithmetic and copies ran while one was open for 27% of the time, Pallas kernels for 0%

profile of v3, /device:TPU:0, one launch (start us, length us, event | category | flops | bytes accessed | tf_op | source)
XLA Modules:
  0.0 150.5 jit_solution(18291378920094989701)
XLA Ops:
  0.7 2.3 %dynamic-slice_convert_fusion.1 = bf16[320,896]{1,0:T(8,128)(2,1)} fusion(f32[320,1792]{1,0:T(8,128)} %param.8, s32[]{:T(128)S(6)} %select_n.265), kind=kLoop, calls=%fused_computation.51 | loop fusion | bytes 1146884 | tf_op jit(solution)/shard_map/convert_element_type | solution.py:108
  2.9 3.0 %collective-permute-start.2 = (bf16[320,896]{1,0:T(8,128)(2,1)}, bf16[320,896]{1,0:T(8,128)(2,1)}, u32[]{:S(2)}, u32[]{:S(2)}) collective-permute-start(bf16[320,896]{1,0:T(8,128)(2,1)} %dynamic-slice_convert_fusion.1), channel_id=1, source_target_pairs={{0,4},{4,0},{1,5},{5,1},{2,6},{6,2},{3,7},{7,3},{8,12},{12,8},{9,1... | collective-permute-start | bytes 1720328 | tf_op jit(solution)/shard_map/ppermute | solution.py:102
  7.4 2.0 %constant_dynamic-slice_fusion.4 = (bf16[128,1280]{1,0:T(8,128)(2,1)}, bf16[128,1280]{1,0:T(8,128)(2,1)}) fusion(bf16[128,2560]{1,0:T(8,128)(2,1)} %param.5, s32[]{:T(128)S(6)} %select_n.289, s32[]{:T(128)S(6)} %select_n.281), kind=kLoop, calls=%fused_computation.101 | loop fusion | bytes 1310728 | tf_op jit(solution)/shard_map/dynamic_slice | solution.py:99
  9.9 2.1 %dynamic-slice_convert_fusion = bf16[320,896]{1,0:T(8,128)(2,1)} fusion(f32[320,1792]{1,0:T(8,128)} %param.8, s32[]{:T(128)S(6)} %select_n.271), kind=kLoop, calls=%fused_computation.50 | loop fusion | bytes 1146884 | tf_op jit(solution)/shard_map/convert_element_type | solution.py:108
  12.0 3.8 %fusion.13 = bf16[512,1792]{1,0:T(8,128)(2,1)} fusion(bf16[512,1792]{1,0:T(8,128)(2,1)} %param.7, bf16[512,1792]{1,0:T(8,128)(2,1)S(1)} %copy-done.2), kind=kLoop, calls=%fused_computation.19 | loop fusion | flops 7340032 | bytes 5505024 | tf_op jit(solution)/shard_map/convert_element_type | solution.py:134
  17.0 1.9 %constant_dynamic-slice_fusion.8 = bf16[512,512]{1,0:T(8,128)(2,1)} fusion(bf16[512,1792]{1,0:T(8,128)(2,1)} %fusion.13, s32[]{:T(128)S(6)} %select_n.265), kind=kLoop, calls=%fused_computation.106 | loop fusion | bytes 1048580 | tf_op jit(solution)/shard_map/dynamic_slice | solution.py:99
  21.7 2.0 %collective-permute-start.3 = (bf16[640,896]{1,0:T(8,128)(2,1)S(1)}, bf16[640,896]{1,0:T(8,128)(2,1)S(1)}, u32[]{:S(2)}, u32[]{:S(2)}) collective-permute-start(bf16[640,896]{1,0:T(8,128)(2,1)S(1)} %maximum_select_fusion.2), channel_id=1, source_target_pairs={{0,8},{16,24},{8,0},{24,16},{1,9},{17,25},{9,1},{25,17},{2,10},{18... | collective-permute-start | bytes 3440648 | tf_op jit(solution)/shard_map/ppermute | solution.py:126
  31.9 3.4 %collective-permute-done.6 = bf16[128,1280]{1,0:T(8,128)(2,1)S(1)} collective-permute-done((bf16[128,1280]{1,0:T(8,128)(2,1)}, bf16[128,1280]{1,0:T(8,128)(2,1)S(1)}, u32[]{:S(2)}, u32[]{:S(2)}) %collective-permute-start.6) | collective-permute-done | bytes 327712 | tf_op jit(solution)/shard_map/ppermute | solution.py:102
  37.5 2.9 %collective-permute-done.8 = bf16[512,512]{1,0:T(8,128)(2,1)S(1)} collective-permute-done((bf16[512,512]{1,0:T(8,128)(2,1)S(1)}, bf16[512,512]{1,0:T(8,128)(2,1)S(1)}, u32[]{:S(2)}, u32[]{:S(2)}) %collective-permute-start.8) | collective-permute-done | bytes 524320 | tf_op jit(solution)/shard_map/ppermute | solution.py:102
  45.9 3.5 %collective-permute-start.13 = (bf16[640,512]{1,0:T(8,128)(2,1)S(1)}, bf16[640,512]{1,0:T(8,128)(2,1)S(1)}, u32[]{:S(2)}, u32[]{:S(2)}) collective-permute-start(bf16[640,512]{1,0:T(8,128)(2,1)S(1)} %get-tuple-element.83), channel_id=1, source_target_pairs={{0,8},{24,16},{1,9},{25,17},{2,10},{26,18},{3,11},{27,19},{4,12},{... | collective-permute-start | bytes 1966088 | tf_op jit(solution)/shard_map/ppermute | solution.py:216
  54.6 4.1 %collective-permute-done.15 = bf16[128,1280]{1,0:T(8,128)(2,1)S(1)} collective-permute-done((bf16[128,1280]{1,0:T(8,128)(2,1)S(1)}, bf16[128,1280]{1,0:T(8,128)(2,1)S(1)}, u32[]{:S(2)}, u32[]{:S(2)}) %collective-permute-start.15) | collective-permute-done | bytes 327712 | tf_op jit(solution)/shard_map/ppermute | solution.py:102
  58.6 5.2 %collective-permute-start.19 = (bf16[640,512]{1,0:T(8,128)(2,1)S(1)}, bf16[640,512]{1,0:T(8,128)(2,1)S(1)}, u32[]{:S(2)}, u32[]{:S(2)}) collective-permute-start(bf16[640,512]{1,0:T(8,128)(2,1)S(1)} %get-tuple-element.51), channel_id=1, source_target_pairs={{0,8},{24,16},{1,9},{25,17},{2,10},{26,18},{3,11},{27,19},{4,12},{... | collective-permute-start | bytes 1966088 | tf_op jit(solution)/shard_map/ppermute | solution.py:216
  66.9 5.8 %collective-permute-start.21 = (bf16[1280,384]{1,0:T(8,128)(2,1)S(1)}, bf16[1280,384]{1,0:T(8,128)(2,1)S(1)}, u32[]{:S(2)}, u32[]{:S(2)}) collective-permute-start(bf16[1280,384]{1,0:T(8,128)(2,1)S(1)} %fusion.20), channel_id=1, source_target_pairs={{0,8},{24,16},{1,9},{25,17},{2,10},{26,18},{3,11},{27,19},{4,12},{... | collective-permute-start | bytes 2949128 | tf_op jit(solution)/shard_map/ppermute | solution.py:227
  83.8 14.0 %collective-permute-start.20 = (bf16[640,512]{1,0:T(8,128)(2,1)S(1)}, bf16[640,512]{1,0:T(8,128)(2,1)S(1)}, u32[]{:S(2)}, u32[]{:S(2)}) collective-permute-start(bf16[640,512]{1,0:T(8,128)(2,1)S(1)} %get-tuple-element.62), channel_id=1, source_target_pairs={{0,8},{16,24},{8,0},{24,16},{1,9},{17,25},{9,1},{25,17},{2,10},{18... | collective-permute-start | bytes 1966088 | tf_op jit(solution)/shard_map/ppermute | solution.py:216
  98.7 9.3 %collective-permute-done.14 = bf16[640,896]{1,0:T(8,128)(2,1)S(1)} collective-permute-done((bf16[640,896]{1,0:T(8,128)(2,1)S(1)}, bf16[640,896]{1,0:T(8,128)(2,1)S(1)}, u32[]{:S(2)}, u32[]{:S(2)}) %collective-permute-start.14) | collective-permute-done | bytes 1146912 | tf_op jit(solution)/shard_map/ppermute | solution.py:126
  109.1 2.1 %collective-permute-start.17 = (bf16[512,896]{1,0:T(8,128)(2,1)S(1)}, bf16[512,896]{1,0:T(8,128)(2,1)S(1)}, u32[]{:S(2)}, u32[]{:S(2)}) collective-permute-start(bf16[512,896]{1,0:T(8,128)(2,1)S(1)} %multiply_convert_fusion), channel_id=1, source_target_pairs={{0,4},{4,0},{1,5},{5,1},{2,6},{6,2},{3,7},{7,3},{8,12},{12,8},{9,1... | collective-permute-start | bytes 2752520 | tf_op jit(solution)/shard_map/ppermute | solution.py:102
  112.9 7.9 %collective-permute-start.24 = (bf16[640,384]{1,0:T(8,128)(2,1)S(1)}, bf16[640,384]{1,0:T(8,128)(2,1)S(1)}, u32[]{:S(2)}, u32[]{:S(2)}) collective-permute-start(bf16[640,384]{1,0:T(8,128)(2,1)S(1)} %get-tuple-element.64), channel_id=1, source_target_pairs={{0,8},{16,24},{8,0},{24,16},{1,9},{17,25},{9,1},{25,17},{2,10},{18... | collective-permute-start | bytes 1474568 | tf_op jit(solution)/shard_map/ppermute | solution.py:216
  122.6 2.1 %collective-permute-start.26 = (bf16[320,512]{1,0:T(8,128)(2,1)S(1)}, bf16[320,512]{1,0:T(8,128)(2,1)S(1)}, u32[]{:S(2)}, u32[]{:S(2)}) collective-permute-start(bf16[320,512]{1,0:T(8,128)(2,1)S(1)} %constant_dynamic-slice_fusion.1), channel_id=1, source_target_pairs={{0,4},{4,0},{1,5},{5,1},{2,6},{6,2},{3,7},{7,3},{8,12},{12,8},{9,1... | collective-permute-start | bytes 983048 | tf_op jit(solution)/shard_map/ppermute | solution.py:102
  124.8 6.7 %collective-permute-done.24 = bf16[640,384]{1,0:T(8,128)(2,1)S(1)} collective-permute-done((bf16[640,384]{1,0:T(8,128)(2,1)S(1)}, bf16[640,384]{1,0:T(8,128)(2,1)S(1)}, u32[]{:S(2)}, u32[]{:S(2)}) %collective-permute-start.24) | collective-permute-done | bytes 491552 | tf_op jit(solution)/shard_map/ppermute | solution.py:216
  132.9 2.1 %collective-permute-start.27 = (bf16[320,384]{1,0:T(8,128)(2,1)S(1)}, bf16[320,384]{1,0:T(8,128)(2,1)S(1)}, u32[]{:S(2)}, u32[]{:S(2)}) collective-permute-start(bf16[320,384]{1,0:T(8,128)(2,1)S(1)} %constant_dynamic-slice_fusion.2), channel_id=1, source_target_pairs={{0,4},{4,0},{1,5},{5,1},{2,6},{6,2},{3,7},{7,3},{8,12},{12,8},{9,1... | collective-permute-start | bytes 737288 | tf_op jit(solution)/shard_map/ppermute | solution.py:102
  134.9 4.5 %collective-permute-done.26 = bf16[320,512]{1,0:T(8,128)(2,1)S(1)} collective-permute-done((bf16[320,512]{1,0:T(8,128)(2,1)S(1)}, bf16[320,512]{1,0:T(8,128)(2,1)S(1)}, u32[]{:S(2)}, u32[]{:S(2)}) %collective-permute-start.26) | collective-permute-done | bytes 327712 | tf_op jit(solution)/shard_map/ppermute | solution.py:102
  139.7 2.3 %collective-permute-done.27 = bf16[320,384]{1,0:T(8,128)(2,1)S(1)} collective-permute-done((bf16[320,384]{1,0:T(8,128)(2,1)S(1)}, bf16[320,384]{1,0:T(8,128)(2,1)S(1)}, u32[]{:S(2)}, u32[]{:S(2)}) %collective-permute-start.27) | collective-permute-done | bytes 245792 | tf_op jit(solution)/shard_map/ppermute | solution.py:102
  144.4 3.4 %fusion.12 = (bf16[512,1792]{1,0:T(8,128)(2,1)}, bf16[512,1792]{1,0:T(8,128)(2,1)}) fusion(bf16[512,1792]{1,0:T(8,128)(2,1)S(1)} %copy-done.3, bf16[512,896]{1,0:T(8,128)(2,1)S(1)} %multiply_convert_fusion.1, bf16[512,896]{1,0:T(8,128)(2,1)S(1)} %collective-permute-done.17, pred[]{:T(512)S(6)} %eq.51, bf16[512,1792]{1,0:T(8,128)(2,1)S(1)} %copy-done.4), kind=kLoop, calls=%fused_computation.18 | loop fusion | flops 22937600 | bytes 9175041 | tf_op jit(solution)/shard_map/convert_element_type | solution.py:272
  147.9 2.6 %multiply_subtract_fusion = (f32[320,1792]{1,0:T(8,128)}, f32[320,1792]{1,0:T(8,128)}) fusion(f32[320,1792]{1,0:T(8,128)S(1)} %copy-done, f32[320]{0:T(512)S(1)} %minimum_reduce_fusion, bf16[320,384]{1,0:T(8,128)(2,1)S(1)} %get-tuple-element.73, bf16[320,512]{1,0:T(8,128)(2,1)S(1)} %get-tuple-element.71, bf16[320,384]{1,0:T(8,128)(2,1)S(1)} %collective-permute-done.27, ...), kind=kLoop, calls=%fused_computation.33 | loop fusion | flops 13189120 | bytes 10323201 | tf_op jit(solution)/shard_map/sub | solution.py:307
  (122 shorter events, 50.4 us)
Async XLA Ops:
  2.9 17.2 %collective-permute-start.2 = (bf16[320,896]{1,0:T(8,128)(2,1)}, bf16[320,896]{1,0:T(8,128)(2,1)}, u32[]{:S(2)}, u32[]{:S(2)}) collective-permute-start(bf16[320,896]{1,0:T(8,128)(2,1)} %dynamic-slice_convert_fusion.1), channel_id=1, source_target_pairs={{0,4},{4,0},{1,5},{5,1},{2,6},{6,2},{3,7},{7,3},{8,12},{12,8},{9,1... | collective-permute-start | bytes 1720328 | tf_op jit(solution)/shard_map/ppermute | solution.py:102
  5.9 23.6 %collective-permute-start = (bf16[128,2560]{1,0:T(8,128)(2,1)}, bf16[128,2560]{1,0:T(8,128)(2,1)}, u32[]{:S(2)}, u32[]{:S(2)}) collective-permute-start(bf16[128,2560]{1,0:T(8,128)(2,1)} %param.5), channel_id=1, source_target_pairs={{0,2},{2,0},{1,3},{3,1},{4,6},{6,4},{5,7},{7,5},{8,10},{10,8},{9,1... | collective-permute-start | bytes 1966088 | tf_op jit(solution)/shard_map/ppermute | solution.py:102
  9.4 16.8 %collective-permute-start.5 = (bf16[128,1280]{1,0:T(8,128)(2,1)}, bf16[128,1280]{1,0:T(8,128)(2,1)}, u32[]{:S(2)}, u32[]{:S(2)}) collective-permute-start(bf16[128,1280]{1,0:T(8,128)(2,1)} %get-tuple-element.41), channel_id=1, source_target_pairs={{0,4},{4,0},{1,5},{5,1},{2,6},{6,2},{3,7},{7,3},{8,12},{12,8},{9,1... | collective-permute-start | bytes 983048 | tf_op jit(solution)/shard_map/ppermute | solution.py:102
  21.7 27.7 %collective-permute-start.3 = (bf16[640,896]{1,0:T(8,128)(2,1)S(1)}, bf16[640,896]{1,0:T(8,128)(2,1)S(1)}, u32[]{:S(2)}, u32[]{:S(2)}) collective-permute-start(bf16[640,896]{1,0:T(8,128)(2,1)S(1)} %maximum_select_fusion.2), channel_id=1, source_target_pairs={{0,8},{16,24},{8,0},{24,16},{1,9},{17,25},{9,1},{25,17},{2,10},{18... | collective-permute-start | bytes 3440648 | tf_op jit(solution)/shard_map/ppermute | solution.py:126
  23.8 26.4 %collective-permute-start.4 = (bf16[640,896]{1,0:T(8,128)(2,1)S(1)}, bf16[640,896]{1,0:T(8,128)(2,1)S(1)}, u32[]{:S(2)}, u32[]{:S(2)}) collective-permute-start(bf16[640,896]{1,0:T(8,128)(2,1)S(1)} %maximum_select_fusion.2), channel_id=1, source_target_pairs={{8,16},{16,8},{9,17},{17,9},{10,18},{18,10},{11,19},{19,11},{12,20... | collective-permute-start | bytes 3440648 | tf_op jit(solution)/shard_map/ppermute | solution.py:126
  27.9 12.5 %collective-permute-start.8 = (bf16[512,512]{1,0:T(8,128)(2,1)S(1)}, bf16[512,512]{1,0:T(8,128)(2,1)S(1)}, u32[]{:S(2)}, u32[]{:S(2)}) collective-permute-start(bf16[512,512]{1,0:T(8,128)(2,1)S(1)} %copy-done.8), channel_id=1, source_target_pairs={{0,4},{4,0},{1,5},{5,1},{2,6},{6,2},{3,7},{7,3},{8,12},{12,8},{9,1... | collective-permute-start | bytes 1572872 | tf_op jit(solution)/shard_map/ppermute | solution.py:102
  30.6 12.6 %collective-permute-start.1 = (bf16[256,2560]{1,0:T(8,128)(2,1)S(1)}, bf16[256,2560]{1,0:T(8,128)(2,1)S(1)}, u32[]{:S(2)}, u32[]{:S(2)}) collective-permute-start(bf16[256,2560]{1,0:T(8,128)(2,1)S(1)} %pad_maximum_fusion), channel_id=1, source_target_pairs={{0,1},{1,0},{2,3},{3,2},{4,5},{5,4},{6,7},{7,6},{8,9},{9,8},{10,11... | collective-permute-start | bytes 3932168 | tf_op jit(solution)/shard_map/ppermute | solution.py:149
  40.4 11.1 %collective-permute-start.11 = (bf16[128,1280]{1,0:T(8,128)(2,1)S(1)}, bf16[128,1280]{1,0:T(8,128)(2,1)S(1)}, u32[]{:S(2)}, u32[]{:S(2)}) collective-permute-start(bf16[128,1280]{1,0:T(8,128)(2,1)S(1)} %copy-done.9), channel_id=1, source_target_pairs={{0,4},{4,0},{1,5},{5,1},{2,6},{6,2},{3,7},{7,3},{8,12},{12,8},{9,1... | collective-permute-start | bytes 983048 | tf_op jit(solution)/shard_map/ppermute | solution.py:102
  45.9 20.0 %collective-permute-start.13 = (bf16[640,512]{1,0:T(8,128)(2,1)S(1)}, bf16[640,512]{1,0:T(8,128)(2,1)S(1)}, u32[]{:S(2)}, u32[]{:S(2)}) collective-permute-start(bf16[640,512]{1,0:T(8,128)(2,1)S(1)} %get-tuple-element.83), channel_id=1, source_target_pairs={{0,8},{24,16},{1,9},{25,17},{2,10},{26,18},{3,11},{27,19},{4,12},{... | collective-permute-start | bytes 1966088 | tf_op jit(solution)/shard_map/ppermute | solution.py:216
  49.4 28.5 %collective-permute-start.10 = (bf16[640,896]{1,0:T(8,128)(2,1)S(1)}, bf16[640,896]{1,0:T(8,128)(2,1)S(1)}, u32[]{:S(2)}, u32[]{:S(2)}) collective-permute-start(bf16[640,896]{1,0:T(8,128)(2,1)S(1)} %collective-permute-done.3), channel_id=1, source_target_pairs={{8,16},{16,8},{9,17},{17,9},{10,18},{18,10},{11,19},{19,11},{12,20... | collective-permute-start | bytes 3440648 | tf_op jit(solution)/shard_map/ppermute | solution.py:126
  50.2 31.6 %collective-permute-start.9 = (bf16[640,896]{1,0:T(8,128)(2,1)S(1)}, bf16[640,896]{1,0:T(8,128)(2,1)S(1)}, u32[]{:S(2)}, u32[]{:S(2)}) collective-permute-start(bf16[640,896]{1,0:T(8,128)(2,1)S(1)} %collective-permute-done.4), channel_id=1, source_target_pairs={{16,24},{8,0},{17,25},{9,1},{18,26},{10,2},{19,27},{11,3},{20,28},... | collective-permute-start | bytes 3440648 | tf_op jit(solution)/shard_map/ppermute | solution.py:126
  53.0 11.0 %collective-permute-start.12 = (bf16[512,384]{1,0:T(8,128)(2,1)S(1)}, bf16[512,384]{1,0:T(8,128)(2,1)S(1)}, u32[]{:S(2)}, u32[]{:S(2)}) collective-permute-start(bf16[512,384]{1,0:T(8,128)(2,1)S(1)} %get-tuple-element.50), channel_id=1, source_target_pairs={{0,4},{4,0},{1,5},{5,1},{2,6},{6,2},{3,7},{7,3},{8,12},{12,8},{9,1... | collective-permute-start | bytes 1179656 | tf_op jit(solution)/shard_map/ppermute | solution.py:102
  58.6 21.6 %collective-permute-start.19 = (bf16[640,512]{1,0:T(8,128)(2,1)S(1)}, bf16[640,512]{1,0:T(8,128)(2,1)S(1)}, u32[]{:S(2)}, u32[]{:S(2)}) collective-permute-start(bf16[640,512]{1,0:T(8,128)(2,1)S(1)} %get-tuple-element.51), channel_id=1, source_target_pairs={{0,8},{24,16},{1,9},{25,17},{2,10},{26,18},{3,11},{27,19},{4,12},{... | collective-permute-start | bytes 1966088 | tf_op jit(solution)/shard_map/ppermute | solution.py:216
  66.2 14.0 %collective-permute-start.18 = (bf16[640,512]{1,0:T(8,128)(2,1)S(1)}, bf16[640,512]{1,0:T(8,128)(2,1)S(1)}, u32[]{:S(2)}, u32[]{:S(2)}) collective-permute-start(bf16[640,512]{1,0:T(8,128)(2,1)S(1)} %add_convert_fusion.3), channel_id=1, source_target_pairs={{8,16},{16,8},{9,17},{17,9},{10,18},{18,10},{11,19},{19,11},{12,20... | collective-permute-start | bytes 1966088 | tf_op jit(solution)/shard_map/ppermute | solution.py:216
  66.9 30.9 %collective-permute-start.21 = (bf16[1280,384]{1,0:T(8,128)(2,1)S(1)}, bf16[1280,384]{1,0:T(8,128)(2,1)S(1)}, u32[]{:S(2)}, u32[]{:S(2)}) collective-permute-start(bf16[1280,384]{1,0:T(8,128)(2,1)S(1)} %fusion.20), channel_id=1, source_target_pairs={{0,8},{24,16},{1,9},{25,17},{2,10},{26,18},{3,11},{27,19},{4,12},{... | collective-permute-start | bytes 2949128 | tf_op jit(solution)/shard_map/ppermute | solution.py:227
  77.9 30.0 %collective-permute-start.14 = (bf16[640,896]{1,0:T(8,128)(2,1)S(1)}, bf16[640,896]{1,0:T(8,128)(2,1)S(1)}, u32[]{:S(2)}, u32[]{:S(2)}) collective-permute-start(bf16[640,896]{1,0:T(8,128)(2,1)S(1)} %collective-permute-done.10), channel_id=1, source_target_pairs={{16,24},{8,0},{17,25},{9,1},{18,26},{10,2},{19,27},{11,3},{20,28},... | collective-permute-start | bytes 3440648 | tf_op jit(solution)/shard_map/ppermute | solution.py:126
  81.1 16.9 %collective-permute-start.22 = (bf16[640,512]{1,0:T(8,128)(2,1)S(1)}, bf16[640,512]{1,0:T(8,128)(2,1)S(1)}, u32[]{:S(2)}, u32[]{:S(2)}) collective-permute-start(bf16[640,512]{1,0:T(8,128)(2,1)S(1)} %get-tuple-element.60), channel_id=1, source_target_pairs={{8,16},{16,8},{9,17},{17,9},{10,18},{18,10},{11,19},{19,11},{12,20... | collective-permute-start | bytes 1966088 | tf_op jit(solution)/shard_map/ppermute | solution.py:216
  83.8 38.2 %collective-permute-start.20 = (bf16[640,512]{1,0:T(8,128)(2,1)S(1)}, bf16[640,512]{1,0:T(8,128)(2,1)S(1)}, u32[]{:S(2)}, u32[]{:S(2)}) collective-permute-start(bf16[640,512]{1,0:T(8,128)(2,1)S(1)} %get-tuple-element.62), channel_id=1, source_target_pairs={{0,8},{16,24},{8,0},{24,16},{1,9},{17,25},{9,1},{25,17},{2,10},{18... | collective-permute-start | bytes 1966088 | tf_op jit(solution)/shard_map/ppermute | solution.py:216
  98.0 14.2 %collective-permute-start.23 = (bf16[640,384]{1,0:T(8,128)(2,1)S(1)}, bf16[640,384]{1,0:T(8,128)(2,1)S(1)}, u32[]{:S(2)}, u32[]{:S(2)}) collective-permute-start(bf16[640,384]{1,0:T(8,128)(2,1)S(1)} %add_convert_fusion.6), channel_id=1, source_target_pairs={{8,16},{16,8},{9,17},{17,9},{10,18},{18,10},{11,19},{19,11},{12,20... | collective-permute-start | bytes 1474568 | tf_op jit(solution)/shard_map/ppermute | solution.py:216
  109.1 23.4 %collective-permute-start.17 = (bf16[512,896]{1,0:T(8,128)(2,1)S(1)}, bf16[512,896]{1,0:T(8,128)(2,1)S(1)}, u32[]{:S(2)}, u32[]{:S(2)}) collective-permute-start(bf16[512,896]{1,0:T(8,128)(2,1)S(1)} %multiply_convert_fusion), channel_id=1, source_target_pairs={{0,4},{4,0},{1,5},{5,1},{2,6},{6,2},{3,7},{7,3},{8,12},{12,8},{9,1... | collective-permute-start | bytes 2752520 | tf_op jit(solution)/shard_map/ppermute | solution.py:102
  112.9 18.6 %collective-permute-start.24 = (bf16[640,384]{1,0:T(8,128)(2,1)S(1)}, bf16[640,384]{1,0:T(8,128)(2,1)S(1)}, u32[]{:S(2)}, u32[]{:S(2)}) collective-permute-start(bf16[640,384]{1,0:T(8,128)(2,1)S(1)} %get-tuple-element.64), channel_id=1, source_target_pairs={{0,8},{16,24},{8,0},{24,16},{1,9},{17,25},{9,1},{25,17},{2,10},{18... | collective-permute-start | bytes 1474568 | tf_op jit(solution)/shard_map/ppermute | solution.py:216
  120.8 11.6 %collective-permute-start.25 = (bf16[640,384]{1,0:T(8,128)(2,1)S(1)}, bf16[640,384]{1,0:T(8,128)(2,1)S(1)}, u32[]{:S(2)}, u32[]{:S(2)}) collective-permute-start(bf16[640,384]{1,0:T(8,128)(2,1)S(1)} %get-tuple-element.65), channel_id=1, source_target_pairs={{8,16},{16,8},{9,17},{17,9},{10,18},{18,10},{11,19},{19,11},{12,20... | collective-permute-start | bytes 1474568 | tf_op jit(solution)/shard_map/ppermute | solution.py:216
  122.6 16.8 %collective-permute-start.26 = (bf16[320,512]{1,0:T(8,128)(2,1)S(1)}, bf16[320,512]{1,0:T(8,128)(2,1)S(1)}, u32[]{:S(2)}, u32[]{:S(2)}) collective-permute-start(bf16[320,512]{1,0:T(8,128)(2,1)S(1)} %constant_dynamic-slice_fusion.1), channel_id=1, source_target_pairs={{0,4},{4,0},{1,5},{5,1},{2,6},{6,2},{3,7},{7,3},{8,12},{12,8},{9,1... | collective-permute-start | bytes 983048 | tf_op jit(solution)/shard_map/ppermute | solution.py:102
  132.9 9.1 %collective-permute-start.27 = (bf16[320,384]{1,0:T(8,128)(2,1)S(1)}, bf16[320,384]{1,0:T(8,128)(2,1)S(1)}, u32[]{:S(2)}, u32[]{:S(2)}) collective-permute-start(bf16[320,384]{1,0:T(8,128)(2,1)S(1)} %constant_dynamic-slice_fusion.2), channel_id=1, source_target_pairs={{0,4},{4,0},{1,5},{5,1},{2,6},{6,2},{3,7},{7,3},{8,12},{12,8},{9,1... | collective-permute-start | bytes 737288 | tf_op jit(solution)/shard_map/ppermute | solution.py:102
  (17 other events, 128.9 us)

commit v4 on v3

--- a/solution.py
+++ b/solution.py
@@ -9,7 +9,7 @@
     "ow": ["gw"],
     "x": ["gw"],
     "h": ["ow"],
-    "d1": ["gw"],
+    "d1": ["h"],
     "sa": ["y1", "sh"],
     "d2": ["ta"],
     "sb": ["y2", "S1Ea"],

time: 151 us -> 151 us (level)
  waiting for transfers between devices: 36.1 us -> 39.5 us
  local copies, waits for them, and re-layouts: 15.1 us -> 13.2 us
    ppermute x8, starting transfers between devices: 33.6 us -> 31.6 us  [reduce(): lax.ppermute(v, 'z', pairs)]
    ppermute x11, waiting for transfers between devices: 19.8 us -> 21.6 us  [over(): return lambda value: lax.ppermute(value, axis, SWAP)]
  transfers between devices with their start and end apart: 31 -> 31, of which waited for: 10 -> 12; matrix products, arithmetic and copies ran while one was open for 27% -> 26% of each run, Pallas kernels for 0% -> 0%
where the time goes in v4:
time: 151 us; the launch traced here: 150 us
  starting transfers between devices  63.5 us (42%)
  waiting for transfers between devices  39.5 us (26%)
  other arithmetic  18.1 us (12%)
  matrix products  15 us (10%)
  local copies, waits for them, and re-layouts  13.2 us (9%)
    ppermute x8, starting transfers between devices, reduce(): lax.ppermute(v, 'z', pairs)  31.6 us
    ppermute x11, waiting for transfers between devices, over(): return lambda value: lax.ppermute(value, axis, SWAP)  21.6 us
    ppermute x11, starting transfers between devices, over(): return lambda value: lax.ppermute(value, axis, SWAP)  17 us
    ppermute x5, waiting for transfers between devices, gather(): g.rule(got, lambda: g[name], lambda v: lax.ppermute(v, 'z', pairs))  9.8 us
    ppermute x8, waiting for transfers between devices, reduce(): lax.ppermute(v, 'z', pairs)  7.77 us
    ppermute x5, starting transfers between devices, gather(): g.rule(got, lambda: g[name], lambda v: lax.ppermute(v, 'z', pairs))  6.22 us
    ppermute x1, starting transfers between devices, first_two(): g.rule('U' + p, lambda: g['S1E' + p], lambda v: lax.ppermute(v, 'z', pairs))  6.2 us
    dot_general x6, matrix products, d_hidden_of(): jnp.dot(columns(tokens, place % n * height, height), piece, preferred_ele...  6.04 us
  transfers between devices with their start and end apart: 31, of which 12 were waited for; matrix products, arithmetic and copies ran while one was open for 26% of the time, Pallas kernels for 0%

profile of v4, /device:TPU:0, one launch (start us, length us, event | category | flops | bytes accessed | tf_op | source)
XLA Modules:
  0.0 150.5 jit_solution(2888453028607500809)
XLA Ops:
  0.7 2.3 %dynamic-slice_convert_fusion.1 = bf16[320,896]{1,0:T(8,128)(2,1)} fusion(f32[320,1792]{1,0:T(8,128)} %param.8, s32[]{:T(128)S(6)} %select_n.265), kind=kLoop, calls=%fused_computation.51 | loop fusion | bytes 1146884 | tf_op jit(solution)/shard_map/convert_element_type | solution.py:108
  2.9 3.0 %collective-permute-start.2 = (bf16[320,896]{1,0:T(8,128)(2,1)}, bf16[320,896]{1,0:T(8,128)(2,1)}, u32[]{:S(2)}, u32[]{:S(2)}) collective-permute-start(bf16[320,896]{1,0:T(8,128)(2,1)} %dynamic-slice_convert_fusion.1), channel_id=1, source_target_pairs={{0,4},{4,0},{1,5},{5,1},{2,6},{6,2},{3,7},{7,3},{8,12},{12,8},{9,1... | collective-permute-start | bytes 1720328 | tf_op jit(solution)/shard_map/ppermute | solution.py:102
  7.4 2.1 %dynamic-slice_convert_fusion = bf16[320,896]{1,0:T(8,128)(2,1)} fusion(f32[320,1792]{1,0:T(8,128)} %param.8, s32[]{:T(128)S(6)} %select_n.271), kind=kLoop, calls=%fused_computation.50 | loop fusion | bytes 1146884 | tf_op jit(solution)/shard_map/convert_element_type | solution.py:108
  10.5 3.8 %fusion.13 = bf16[512,1792]{1,0:T(8,128)(2,1)} fusion(bf16[512,1792]{1,0:T(8,128)(2,1)} %param.7, bf16[512,1792]{1,0:T(8,128)(2,1)S(1)} %copy-done.2), kind=kLoop, calls=%fused_computation.19 | loop fusion | flops 7340032 | bytes 5505024 | tf_op jit(solution)/shard_map/convert_element_type | solution.py:134
  15.0 1.9 %constant_dynamic-slice_fusion.8 = bf16[512,512]{1,0:T(8,128)(2,1)} fusion(bf16[512,1792]{1,0:T(8,128)(2,1)} %fusion.13, s32[]{:T(128)S(6)} %select_n.265), kind=kLoop, calls=%fused_computation.106 | loop fusion | bytes 1048580 | tf_op jit(solution)/shard_map/dynamic_slice | solution.py:99
  18.2 1.8 %collective-permute-done.2 = bf16[320,896]{1,0:T(8,128)(2,1)} collective-permute-done((bf16[320,896]{1,0:T(8,128)(2,1)}, bf16[320,896]{1,0:T(8,128)(2,1)}, u32[]{:S(2)}, u32[]{:S(2)}) %collective-permute-start.2) | collective-permute-done | bytes 573472 | tf_op jit(solution)/shard_map/ppermute | solution.py:102
  21.6 2.2 %collective-permute-start.3 = (bf16[640,896]{1,0:T(8,128)(2,1)S(1)}, bf16[640,896]{1,0:T(8,128)(2,1)S(1)}, u32[]{:S(2)}, u32[]{:S(2)}) collective-permute-start(bf16[640,896]{1,0:T(8,128)(2,1)S(1)} %maximum_select_fusion.2), channel_id=1, source_target_pairs={{0,8},{16,24},{8,0},{24,16},{1,9},{17,25},{9,1},{25,17},{2,10},{18... | collective-permute-start | bytes 3440648 | tf_op jit(solution)/shard_map/ppermute | solution.py:126
  31.9 3.4 %collective-permute-done.6 = bf16[128,1280]{1,0:T(8,128)(2,1)S(1)} collective-permute-done((bf16[128,1280]{1,0:T(8,128)(2,1)}, bf16[128,1280]{1,0:T(8,128)(2,1)S(1)}, u32[]{:S(2)}, u32[]{:S(2)}) %collective-permute-start.6) | collective-permute-done | bytes 327712 | tf_op jit(solution)/shard_map/ppermute | solution.py:102
  37.6 2.9 %collective-permute-done.8 = bf16[512,512]{1,0:T(8,128)(2,1)S(1)} collective-permute-done((bf16[512,512]{1,0:T(8,128)(2,1)S(1)}, bf16[512,512]{1,0:T(8,128)(2,1)S(1)}, u32[]{:S(2)}, u32[]{:S(2)}) %collective-permute-start.8) | collective-permute-done | bytes 524320 | tf_op jit(solution)/shard_map/ppermute | solution.py:102
  45.9 3.5 %collective-permute-start.13 = (bf16[640,512]{1,0:T(8,128)(2,1)S(1)}, bf16[640,512]{1,0:T(8,128)(2,1)S(1)}, u32[]{:S(2)}, u32[]{:S(2)}) collective-permute-start(bf16[640,512]{1,0:T(8,128)(2,1)S(1)} %get-tuple-element.83), channel_id=1, source_target_pairs={{0,8},{24,16},{1,9},{25,17},{2,10},{26,18},{3,11},{27,19},{4,12},{... | collective-permute-start | bytes 1966088 | tf_op jit(solution)/shard_map/ppermute | solution.py:216
  54.6 4.1 %collective-permute-done.15 = bf16[128,1280]{1,0:T(8,128)(2,1)S(1)} collective-permute-done((bf16[128,1280]{1,0:T(8,128)(2,1)S(1)}, bf16[128,1280]{1,0:T(8,128)(2,1)S(1)}, u32[]{:S(2)}, u32[]{:S(2)}) %collective-permute-start.15) | collective-permute-done | bytes 327712 | tf_op jit(solution)/shard_map/ppermute | solution.py:102
  58.7 4.7 %collective-permute-start.19 = (bf16[640,512]{1,0:T(8,128)(2,1)S(1)}, bf16[640,512]{1,0:T(8,128)(2,1)S(1)}, u32[]{:S(2)}, u32[]{:S(2)}) collective-permute-start(bf16[640,512]{1,0:T(8,128)(2,1)S(1)} %get-tuple-element.51), channel_id=1, source_target_pairs={{0,8},{24,16},{1,9},{25,17},{2,10},{26,18},{3,11},{27,19},{4,12},{... | collective-permute-start | bytes 1966088 | tf_op jit(solution)/shard_map/ppermute | solution.py:216
  66.5 6.2 %collective-permute-start.21 = (bf16[1280,384]{1,0:T(8,128)(2,1)S(1)}, bf16[1280,384]{1,0:T(8,128)(2,1)S(1)}, u32[]{:S(2)}, u32[]{:S(2)}) collective-permute-start(bf16[1280,384]{1,0:T(8,128)(2,1)S(1)} %fusion.20), channel_id=1, source_target_pairs={{0,8},{24,16},{1,9},{25,17},{2,10},{26,18},{3,11},{27,19},{4,12},{... | collective-permute-start | bytes 2949128 | tf_op jit(solution)/shard_map/ppermute | solution.py:227
  83.8 13.2 %collective-permute-start.20 = (bf16[640,512]{1,0:T(8,128)(2,1)S(1)}, bf16[640,512]{1,0:T(8,128)(2,1)S(1)}, u32[]{:S(2)}, u32[]{:S(2)}) collective-permute-start(bf16[640,512]{1,0:T(8,128)(2,1)S(1)} %get-tuple-element.62), channel_id=1, source_target_pairs={{0,8},{16,24},{8,0},{24,16},{1,9},{17,25},{9,1},{25,17},{2,10},{18... | collective-permute-start | bytes 1966088 | tf_op jit(solution)/shard_map/ppermute | solution.py:216
  98.2 9.8 %collective-permute-done.14 = bf16[640,896]{1,0:T(8,128)(2,1)S(1)} collective-permute-done((bf16[640,896]{1,0:T(8,128)(2,1)S(1)}, bf16[640,896]{1,0:T(8,128)(2,1)S(1)}, u32[]{:S(2)}, u32[]{:S(2)}) %collective-permute-start.14) | collective-permute-done | bytes 1146912 | tf_op jit(solution)/shard_map/ppermute | solution.py:126
  109.1 2.0 %collective-permute-start.17 = (bf16[512,896]{1,0:T(8,128)(2,1)S(1)}, bf16[512,896]{1,0:T(8,128)(2,1)S(1)}, u32[]{:S(2)}, u32[]{:S(2)}) collective-permute-start(bf16[512,896]{1,0:T(8,128)(2,1)S(1)} %multiply_convert_fusion), channel_id=1, source_target_pairs={{0,4},{4,0},{1,5},{5,1},{2,6},{6,2},{3,7},{7,3},{8,12},{12,8},{9,1... | collective-permute-start | bytes 2752520 | tf_op jit(solution)/shard_map/ppermute | solution.py:102
  112.9 7.2 %collective-permute-start.24 = (bf16[640,384]{1,0:T(8,128)(2,1)S(1)}, bf16[640,384]{1,0:T(8,128)(2,1)S(1)}, u32[]{:S(2)}, u32[]{:S(2)}) collective-permute-start(bf16[640,384]{1,0:T(8,128)(2,1)S(1)} %get-tuple-element.64), channel_id=1, source_target_pairs={{0,8},{16,24},{8,0},{24,16},{1,9},{17,25},{9,1},{25,17},{2,10},{18... | collective-permute-start | bytes 1474568 | tf_op jit(solution)/shard_map/ppermute | solution.py:216
  122.6 2.0 %collective-permute-start.26 = (bf16[320,512]{1,0:T(8,128)(2,1)S(1)}, bf16[320,512]{1,0:T(8,128)(2,1)S(1)}, u32[]{:S(2)}, u32[]{:S(2)}) collective-permute-start(bf16[320,512]{1,0:T(8,128)(2,1)S(1)} %constant_dynamic-slice_fusion.1), channel_id=1, source_target_pairs={{0,4},{4,0},{1,5},{5,1},{2,6},{6,2},{3,7},{7,3},{8,12},{12,8},{9,1... | collective-permute-start | bytes 983048 | tf_op jit(solution)/shard_map/ppermute | solution.py:102
  124.8 6.7 %collective-permute-done.24 = bf16[640,384]{1,0:T(8,128)(2,1)S(1)} collective-permute-done((bf16[640,384]{1,0:T(8,128)(2,1)S(1)}, bf16[640,384]{1,0:T(8,128)(2,1)S(1)}, u32[]{:S(2)}, u32[]{:S(2)}) %collective-permute-start.24) | collective-permute-done | bytes 491552 | tf_op jit(solution)/shard_map/ppermute | solution.py:216
  132.9 2.0 %collective-permute-start.27 = (bf16[320,384]{1,0:T(8,128)(2,1)S(1)}, bf16[320,384]{1,0:T(8,128)(2,1)S(1)}, u32[]{:S(2)}, u32[]{:S(2)}) collective-permute-start(bf16[320,384]{1,0:T(8,128)(2,1)S(1)} %constant_dynamic-slice_fusion.2), channel_id=1, source_target_pairs={{0,4},{4,0},{1,5},{5,1},{2,6},{6,2},{3,7},{7,3},{8,12},{12,8},{9,1... | collective-permute-start | bytes 737288 | tf_op jit(solution)/shard_map/ppermute | solution.py:102
  134.9 4.5 %collective-permute-done.26 = bf16[320,512]{1,0:T(8,128)(2,1)S(1)} collective-permute-done((bf16[320,512]{1,0:T(8,128)(2,1)S(1)}, bf16[320,512]{1,0:T(8,128)(2,1)S(1)}, u32[]{:S(2)}, u32[]{:S(2)}) %collective-permute-start.26) | collective-permute-done | bytes 327712 | tf_op jit(solution)/shard_map/ppermute | solution.py:102
  139.7 2.3 %collective-permute-done.27 = bf16[320,384]{1,0:T(8,128)(2,1)S(1)} collective-permute-done((bf16[320,384]{1,0:T(8,128)(2,1)S(1)}, bf16[320,384]{1,0:T(8,128)(2,1)S(1)}, u32[]{:S(2)}, u32[]{:S(2)}) %collective-permute-start.27) | collective-permute-done | bytes 245792 | tf_op jit(solution)/shard_map/ppermute | solution.py:102
  144.4 3.4 %fusion.12 = (bf16[512,1792]{1,0:T(8,128)(2,1)}, bf16[512,1792]{1,0:T(8,128)(2,1)}) fusion(bf16[512,1792]{1,0:T(8,128)(2,1)S(1)} %copy-done.3, bf16[512,896]{1,0:T(8,128)(2,1)S(1)} %multiply_convert_fusion.1, bf16[512,896]{1,0:T(8,128)(2,1)S(1)} %collective-permute-done.17, pred[]{:T(512)S(6)} %eq.51, bf16[512,1792]{1,0:T(8,128)(2,1)S(1)} %copy-done.4), kind=kLoop, calls=%fused_computation.18 | loop fusion | flops 22937600 | bytes 9175041 | tf_op jit(solution)/shard_map/convert_element_type | solution.py:272
  147.9 2.6 %multiply_subtract_fusion = (f32[320,1792]{1,0:T(8,128)}, f32[320,1792]{1,0:T(8,128)}) fusion(f32[320,1792]{1,0:T(8,128)S(1)} %copy-done, f32[320]{0:T(512)S(1)} %minimum_reduce_fusion, bf16[320,384]{1,0:T(8,128)(2,1)S(1)} %get-tuple-element.73, bf16[320,512]{1,0:T(8,128)(2,1)S(1)} %get-tuple-element.71, bf16[320,384]{1,0:T(8,128)(2,1)S(1)} %collective-permute-done.27, ...), kind=kLoop, calls=%fused_computation.33 | loop fusion | flops 13189120 | bytes 10323201 | tf_op jit(solution)/shard_map/sub | solution.py:307
  (122 shorter events, 51.5 us)
Async XLA Ops:
  2.9 17.1 %collective-permute-start.2 = (bf16[320,896]{1,0:T(8,128)(2,1)}, bf16[320,896]{1,0:T(8,128)(2,1)}, u32[]{:S(2)}, u32[]{:S(2)}) collective-permute-start(bf16[320,896]{1,0:T(8,128)(2,1)} %dynamic-slice_convert_fusion.1), channel_id=1, source_target_pairs={{0,4},{4,0},{1,5},{5,1},{2,6},{6,2},{3,7},{7,3},{8,12},{12,8},{9,1... | collective-permute-start | bytes 1720328 | tf_op jit(solution)/shard_map/ppermute | solution.py:102
  5.9 23.6 %collective-permute-start = (bf16[128,2560]{1,0:T(8,128)(2,1)}, bf16[128,2560]{1,0:T(8,128)(2,1)}, u32[]{:S(2)}, u32[]{:S(2)}) collective-permute-start(bf16[128,2560]{1,0:T(8,128)(2,1)} %param.5), channel_id=1, source_target_pairs={{0,2},{2,0},{1,3},{3,1},{4,6},{6,4},{5,7},{7,5},{8,10},{10,8},{9,1... | collective-permute-start | bytes 1966088 | tf_op jit(solution)/shard_map/ppermute | solution.py:102
  14.3 11.9 %collective-permute-start.5 = (bf16[128,1280]{1,0:T(8,128)(2,1)}, bf16[128,1280]{1,0:T(8,128)(2,1)}, u32[]{:S(2)}, u32[]{:S(2)}) collective-permute-start(bf16[128,1280]{1,0:T(8,128)(2,1)} %get-tuple-element.41), channel_id=1, source_target_pairs={{0,4},{4,0},{1,5},{5,1},{2,6},{6,2},{3,7},{7,3},{8,12},{12,8},{9,1... | collective-permute-start | bytes 983048 | tf_op jit(solution)/shard_map/ppermute | solution.py:102
  21.6 27.8 %collective-permute-start.3 = (bf16[640,896]{1,0:T(8,128)(2,1)S(1)}, bf16[640,896]{1,0:T(8,128)(2,1)S(1)}, u32[]{:S(2)}, u32[]{:S(2)}) collective-permute-start(bf16[640,896]{1,0:T(8,128)(2,1)S(1)} %maximum_select_fusion.2), channel_id=1, source_target_pairs={{0,8},{16,24},{8,0},{24,16},{1,9},{17,25},{9,1},{25,17},{2,10},{18... | collective-permute-start | bytes 3440648 | tf_op jit(solution)/shard_map/ppermute | solution.py:126
  23.8 26.4 %collective-permute-start.4 = (bf16[640,896]{1,0:T(8,128)(2,1)S(1)}, bf16[640,896]{1,0:T(8,128)(2,1)S(1)}, u32[]{:S(2)}, u32[]{:S(2)}) collective-permute-start(bf16[640,896]{1,0:T(8,128)(2,1)S(1)} %maximum_select_fusion.2), channel_id=1, source_target_pairs={{8,16},{16,8},{9,17},{17,9},{10,18},{18,10},{11,19},{19,11},{12,20... | collective-permute-start | bytes 3440648 | tf_op jit(solution)/shard_map/ppermute | solution.py:126
  27.9 12.5 %collective-permute-start.8 = (bf16[512,512]{1,0:T(8,128)(2,1)S(1)}, bf16[512,512]{1,0:T(8,128)(2,1)S(1)}, u32[]{:S(2)}, u32[]{:S(2)}) collective-permute-start(bf16[512,512]{1,0:T(8,128)(2,1)S(1)} %copy-done.8), channel_id=1, source_target_pairs={{0,4},{4,0},{1,5},{5,1},{2,6},{6,2},{3,7},{7,3},{8,12},{12,8},{9,1... | collective-permute-start | bytes 1572872 | tf_op jit(solution)/shard_map/ppermute | solution.py:102
  30.6 12.6 %collective-permute-start.1 = (bf16[256,2560]{1,0:T(8,128)(2,1)S(1)}, bf16[256,2560]{1,0:T(8,128)(2,1)S(1)}, u32[]{:S(2)}, u32[]{:S(2)}) collective-permute-start(bf16[256,2560]{1,0:T(8,128)(2,1)S(1)} %pad_maximum_fusion), channel_id=1, source_target_pairs={{0,1},{1,0},{2,3},{3,2},{4,5},{5,4},{6,7},{7,6},{8,9},{9,8},{10,11... | collective-permute-start | bytes 3932168 | tf_op jit(solution)/shard_map/ppermute | solution.py:149
  40.5 11.1 %collective-permute-start.11 = (bf16[128,1280]{1,0:T(8,128)(2,1)S(1)}, bf16[128,1280]{1,0:T(8,128)(2,1)S(1)}, u32[]{:S(2)}, u32[]{:S(2)}) collective-permute-start(bf16[128,1280]{1,0:T(8,128)(2,1)S(1)} %copy-done.9), channel_id=1, source_target_pairs={{0,4},{4,0},{1,5},{5,1},{2,6},{6,2},{3,7},{7,3},{8,12},{12,8},{9,1... | collective-permute-start | bytes 983048 | tf_op jit(solution)/shard_map/ppermute | solution.py:102
  45.9 19.6 %collective-permute-start.13 = (bf16[640,512]{1,0:T(8,128)(2,1)S(1)}, bf16[640,512]{1,0:T(8,128)(2,1)S(1)}, u32[]{:S(2)}, u32[]{:S(2)}) collective-permute-start(bf16[640,512]{1,0:T(8,128)(2,1)S(1)} %get-tuple-element.83), channel_id=1, source_target_pairs={{0,8},{24,16},{1,9},{25,17},{2,10},{26,18},{3,11},{27,19},{4,12},{... | collective-permute-start | bytes 1966088 | tf_op jit(solution)/shard_map/ppermute | solution.py:216
  49.5 28.5 %collective-permute-start.10 = (bf16[640,896]{1,0:T(8,128)(2,1)S(1)}, bf16[640,896]{1,0:T(8,128)(2,1)S(1)}, u32[]{:S(2)}, u32[]{:S(2)}) collective-permute-start(bf16[640,896]{1,0:T(8,128)(2,1)S(1)} %collective-permute-done.3), channel_id=1, source_target_pairs={{8,16},{16,8},{9,17},{17,9},{10,18},{18,10},{11,19},{19,11},{12,20... | collective-permute-start | bytes 3440648 | tf_op jit(solution)/shard_map/ppermute | solution.py:126
  50.2 31.6 %collective-permute-start.9 = (bf16[640,896]{1,0:T(8,128)(2,1)S(1)}, bf16[640,896]{1,0:T(8,128)(2,1)S(1)}, u32[]{:S(2)}, u32[]{:S(2)}) collective-permute-start(bf16[640,896]{1,0:T(8,128)(2,1)S(1)} %collective-permute-done.4), channel_id=1, source_target_pairs={{16,24},{8,0},{17,25},{9,1},{18,26},{10,2},{19,27},{11,3},{20,28},... | collective-permute-start | bytes 3440648 | tf_op jit(solution)/shard_map/ppermute | solution.py:126
  53.1 10.5 %collective-permute-start.12 = (bf16[512,384]{1,0:T(8,128)(2,1)S(1)}, bf16[512,384]{1,0:T(8,128)(2,1)S(1)}, u32[]{:S(2)}, u32[]{:S(2)}) collective-permute-start(bf16[512,384]{1,0:T(8,128)(2,1)S(1)} %get-tuple-element.50), channel_id=1, source_target_pairs={{0,4},{4,0},{1,5},{5,1},{2,6},{6,2},{3,7},{7,3},{8,12},{12,8},{9,1... | collective-permute-start | bytes 1179656 | tf_op jit(solution)/shard_map/ppermute | solution.py:102
  58.7 21.5 %collective-permute-start.19 = (bf16[640,512]{1,0:T(8,128)(2,1)S(1)}, bf16[640,512]{1,0:T(8,128)(2,1)S(1)}, u32[]{:S(2)}, u32[]{:S(2)}) collective-permute-start(bf16[640,512]{1,0:T(8,128)(2,1)S(1)} %get-tuple-element.51), channel_id=1, source_target_pairs={{0,8},{24,16},{1,9},{25,17},{2,10},{26,18},{3,11},{27,19},{4,12},{... | collective-permute-start | bytes 1966088 | tf_op jit(solution)/shard_map/ppermute | solution.py:216
  65.8 14.5 %collective-permute-start.18 = (bf16[640,512]{1,0:T(8,128)(2,1)S(1)}, bf16[640,512]{1,0:T(8,128)(2,1)S(1)}, u32[]{:S(2)}, u32[]{:S(2)}) collective-permute-start(bf16[640,512]{1,0:T(8,128)(2,1)S(1)} %add_convert_fusion.3), channel_id=1, source_target_pairs={{8,16},{16,8},{9,17},{17,9},{10,18},{18,10},{11,19},{19,11},{12,20... | collective-permute-start | bytes 1966088 | tf_op jit(solution)/shard_map/ppermute | solution.py:216
  66.5 30.8 %collective-permute-start.21 = (bf16[1280,384]{1,0:T(8,128)(2,1)S(1)}, bf16[1280,384]{1,0:T(8,128)(2,1)S(1)}, u32[]{:S(2)}, u32[]{:S(2)}) collective-permute-start(bf16[1280,384]{1,0:T(8,128)(2,1)S(1)} %fusion.20), channel_id=1, source_target_pairs={{0,8},{24,16},{1,9},{25,17},{2,10},{26,18},{3,11},{27,19},{4,12},{... | collective-permute-start | bytes 2949128 | tf_op jit(solution)/shard_map/ppermute | solution.py:227
  78.0 30.0 %collective-permute-start.14 = (bf16[640,896]{1,0:T(8,128)(2,1)S(1)}, bf16[640,896]{1,0:T(8,128)(2,1)S(1)}, u32[]{:S(2)}, u32[]{:S(2)}) collective-permute-start(bf16[640,896]{1,0:T(8,128)(2,1)S(1)} %collective-permute-done.10), channel_id=1, source_target_pairs={{16,24},{8,0},{17,25},{9,1},{18,26},{10,2},{19,27},{11,3},{20,28},... | collective-permute-start | bytes 3440648 | tf_op jit(solution)/shard_map/ppermute | solution.py:126
  81.1 16.4 %collective-permute-start.22 = (bf16[640,512]{1,0:T(8,128)(2,1)S(1)}, bf16[640,512]{1,0:T(8,128)(2,1)S(1)}, u32[]{:S(2)}, u32[]{:S(2)}) collective-permute-start(bf16[640,512]{1,0:T(8,128)(2,1)S(1)} %get-tuple-element.60), channel_id=1, source_target_pairs={{8,16},{16,8},{9,17},{17,9},{10,18},{18,10},{11,19},{19,11},{12,20... | collective-permute-start | bytes 1966088 | tf_op jit(solution)/shard_map/ppermute | solution.py:216
  83.8 38.2 %collective-permute-start.20 = (bf16[640,512]{1,0:T(8,128)(2,1)S(1)}, bf16[640,512]{1,0:T(8,128)(2,1)S(1)}, u32[]{:S(2)}, u32[]{:S(2)}) collective-permute-start(bf16[640,512]{1,0:T(8,128)(2,1)S(1)} %get-tuple-element.62), channel_id=1, source_target_pairs={{0,8},{16,24},{8,0},{24,16},{1,9},{17,25},{9,1},{25,17},{2,10},{18... | collective-permute-start | bytes 1966088 | tf_op jit(solution)/shard_map/ppermute | solution.py:216
  97.5 14.7 %collective-permute-start.23 = (bf16[640,384]{1,0:T(8,128)(2,1)S(1)}, bf16[640,384]{1,0:T(8,128)(2,1)S(1)}, u32[]{:S(2)}, u32[]{:S(2)}) collective-permute-start(bf16[640,384]{1,0:T(8,128)(2,1)S(1)} %add_convert_fusion.6), channel_id=1, source_target_pairs={{8,16},{16,8},{9,17},{17,9},{10,18},{18,10},{11,19},{19,11},{12,20... | collective-permute-start | bytes 1474568 | tf_op jit(solution)/shard_map/ppermute | solution.py:216
  109.1 23.4 %collective-permute-start.17 = (bf16[512,896]{1,0:T(8,128)(2,1)S(1)}, bf16[512,896]{1,0:T(8,128)(2,1)S(1)}, u32[]{:S(2)}, u32[]{:S(2)}) collective-permute-start(bf16[512,896]{1,0:T(8,128)(2,1)S(1)} %multiply_convert_fusion), channel_id=1, source_target_pairs={{0,4},{4,0},{1,5},{5,1},{2,6},{6,2},{3,7},{7,3},{8,12},{12,8},{9,1... | collective-permute-start | bytes 2752520 | tf_op jit(solution)/shard_map/ppermute | solution.py:102
  112.9 18.6 %collective-permute-start.24 = (bf16[640,384]{1,0:T(8,128)(2,1)S(1)}, bf16[640,384]{1,0:T(8,128)(2,1)S(1)}, u32[]{:S(2)}, u32[]{:S(2)}) collective-permute-start(bf16[640,384]{1,0:T(8,128)(2,1)S(1)} %get-tuple-element.64), channel_id=1, source_target_pairs={{0,8},{16,24},{8,0},{24,16},{1,9},{17,25},{9,1},{25,17},{2,10},{18... | collective-permute-start | bytes 1474568 | tf_op jit(solution)/shard_map/ppermute | solution.py:216
  120.1 12.4 %collective-permute-start.25 = (bf16[640,384]{1,0:T(8,128)(2,1)S(1)}, bf16[640,384]{1,0:T(8,128)(2,1)S(1)}, u32[]{:S(2)}, u32[]{:S(2)}) collective-permute-start(bf16[640,384]{1,0:T(8,128)(2,1)S(1)} %get-tuple-element.65), channel_id=1, source_target_pairs={{8,16},{16,8},{9,17},{17,9},{10,18},{18,10},{11,19},{19,11},{12,20... | collective-permute-start | bytes 1474568 | tf_op jit(solution)/shard_map/ppermute | solution.py:216
  122.6 16.8 %collective-permute-start.26 = (bf16[320,512]{1,0:T(8,128)(2,1)S(1)}, bf16[320,512]{1,0:T(8,128)(2,1)S(1)}, u32[]{:S(2)}, u32[]{:S(2)}) collective-permute-start(bf16[320,512]{1,0:T(8,128)(2,1)S(1)} %constant_dynamic-slice_fusion.1), channel_id=1, source_target_pairs={{0,4},{4,0},{1,5},{5,1},{2,6},{6,2},{3,7},{7,3},{8,12},{12,8},{9,1... | collective-permute-start | bytes 983048 | tf_op jit(solution)/shard_map/ppermute | solution.py:102
  132.9 9.1 %collective-permute-start.27 = (bf16[320,384]{1,0:T(8,128)(2,1)S(1)}, bf16[320,384]{1,0:T(8,128)(2,1)S(1)}, u32[]{:S(2)}, u32[]{:S(2)}) collective-permute-start(bf16[320,384]{1,0:T(8,128)(2,1)S(1)} %constant_dynamic-slice_fusion.2), channel_id=1, source_target_pairs={{0,4},{4,0},{1,5},{5,1},{2,6},{6,2},{3,7},{7,3},{8,12},{12,8},{9,1... | collective-permute-start | bytes 737288 | tf_op jit(solution)/shard_map/ppermute | solution.py:102
  (17 other events, 139.2 us)

commit v5 on v4

--- a/solution.py
+++ b/solution.py
@@ -30,9 +30,10 @@
     "w2": ["ta"],
     "q2": ["S1Ea"],
     "o2": ["S1Ea"],
-    "q1": ["sh"],
+    "q1": ["sh", "sa"],
     "o1": ["sh"],
     "G1O": ["G1E"],
+    "va": ["out", "eb"],
 }
 EDGE = "EO"
 
@@ -287,6 +288,7 @@
         g.rule("e" + p, lambda: rows_of(1 - y), same)
         g.rule("f" + p, lambda: g["e" + p], over("y"))
         g.rule("k" + p, lambda: rows_of(y), same)
+        g.rule("v" + p, lambda: g["f" + p], same)
 
     for p in parts:
         total(p)
@@ -295,12 +297,12 @@
         value = g[name].astype(jnp.float32)
         return jnp.sum(value * value, axis=1)
 
-    grad_square = sum(square_sum(kind + p) for p in parts for kind in "kf")
+    grad_square = sum(square_sum(kind + p) for p in parts for kind in "kv")
     squares = plane_sum(jnp.stack([g["w2"], grad_square]))
     factor = jnp.minimum(1.0, 0.1 * jnp.sqrt(squares[0]) / jnp.sqrt(squares[1] + 1e-06))
     grad = in_order(
         jnp.concatenate([g["k" + p] for p in parts], 1),
-        jnp.concatenate([g["f" + p] for p in parts], 1),
+        jnp.concatenate([g["v" + p] for p in parts], 1),
         1,
     ).astype(jnp.float32)
     momentum_new = 0.9 * momentum + grad * factor[:, None]

time: 151 us -> 149 us (0.987)
  waiting for transfers between devices: 39.5 us -> 37.2 us
    ppermute x11, waiting for transfers between devices: 21.6 us -> 17.3 us  [over(): return lambda value: lax.ppermute(value, axis, SWAP)]
  transfers between devices with their start and end apart: 31 -> 31, of which waited for: 12 -> 14; matrix products, arithmetic and copies ran while one was open for 26% -> 27% of each run, Pallas kernels for 0% -> 0%
where the time goes in v5:
time: 149 us
  starting transfers between devices  63.9 us (43%)
  waiting for transfers between devices  37.2 us (25%)
  other arithmetic  18.1 us (12%)
  matrix products  15 us (10%)
  local copies, waits for them, and re-layouts  13.2 us (9%)
    ppermute x8, starting transfers between devices, reduce(): lax.ppermute(v, 'z', pairs)  32.6 us
    ppermute x11, waiting for transfers between devices, over(): return lambda value: lax.ppermute(value, axis, SWAP)  17.3 us
    ppermute x11, starting transfers between devices, over(): return lambda value: lax.ppermute(value, axis, SWAP)  16.5 us
    ppermute x5, waiting for transfers between devices, gather(): g.rule(got, lambda: g[name], lambda v: lax.ppermute(v, 'z', pairs))  9.14 us
    ppermute x8, waiting for transfers between devices, reduce(): lax.ppermute(v, 'z', pairs)  7.9 us
    ppermute x5, starting transfers between devices, gather(): g.rule(got, lambda: g[name], lambda v: lax.ppermute(v, 'z', pairs))  6.22 us
    ppermute x1, starting transfers between devices, first_two(): g.rule('U' + p, lambda: g['S1E' + p], lambda v: lax.ppermute(v, 'z', pairs))  6.2 us
    dot_general x6, matrix products, d_hidden_of(): jnp.dot(columns(tokens, place % n * height, height), piece, preferred_ele...  6.04 us
  transfers between devices with their start and end apart: 31, of which 14 were waited for; matrix products, arithmetic and copies ran while one was open for 27% of the time, Pallas kernels for 0%

profile of v5, /device:TPU:0, one launch (start us, length us, event | category | flops | bytes accessed | tf_op | source)
XLA Modules:
  0.0 148.6 jit_solution(6019460700715012708)
XLA Ops:
  0.7 2.3 %dynamic-slice_convert_fusion.1 = bf16[320,896]{1,0:T(8,128)(2,1)} fusion(f32[320,1792]{1,0:T(8,128)} %param.8, s32[]{:T(128)S(6)} %select_n.265), kind=kLoop, calls=%fused_computation.51 | loop fusion | bytes 1146884 | tf_op jit(solution)/shard_map/convert_element_type | solution.py:109
  2.9 3.0 %collective-permute-start.2 = (bf16[320,896]{1,0:T(8,128)(2,1)}, bf16[320,896]{1,0:T(8,128)(2,1)}, u32[]{:S(2)}, u32[]{:S(2)}) collective-permute-start(bf16[320,896]{1,0:T(8,128)(2,1)} %dynamic-slice_convert_fusion.1), channel_id=1, source_target_pairs={{0,4},{4,0},{1,5},{5,1},{2,6},{6,2},{3,7},{7,3},{8,12},{12,8},{9,1... | collective-permute-start | bytes 1720328 | tf_op jit(solution)/shard_map/ppermute | solution.py:103
  7.4 2.1 %dynamic-slice_convert_fusion = bf16[320,896]{1,0:T(8,128)(2,1)} fusion(f32[320,1792]{1,0:T(8,128)} %param.8, s32[]{:T(128)S(6)} %select_n.271), kind=kLoop, calls=%fused_computation.50 | loop fusion | bytes 1146884 | tf_op jit(solution)/shard_map/convert_element_type | solution.py:109
  10.5 3.8 %fusion.13 = bf16[512,1792]{1,0:T(8,128)(2,1)} fusion(bf16[512,1792]{1,0:T(8,128)(2,1)} %param.7, bf16[512,1792]{1,0:T(8,128)(2,1)S(1)} %copy-done.2), kind=kLoop, calls=%fused_computation.19 | loop fusion | flops 7340032 | bytes 5505024 | tf_op jit(solution)/shard_map/convert_element_type | solution.py:135
  15.0 1.9 %constant_dynamic-slice_fusion.8 = bf16[512,512]{1,0:T(8,128)(2,1)} fusion(bf16[512,1792]{1,0:T(8,128)(2,1)} %fusion.13, s32[]{:T(128)S(6)} %select_n.265), kind=kLoop, calls=%fused_computation.108 | loop fusion | bytes 1048580 | tf_op jit(solution)/shard_map/dynamic_slice | solution.py:100
  18.2 1.8 %collective-permute-done.2 = bf16[320,896]{1,0:T(8,128)(2,1)} collective-permute-done((bf16[320,896]{1,0:T(8,128)(2,1)}, bf16[320,896]{1,0:T(8,128)(2,1)}, u32[]{:S(2)}, u32[]{:S(2)}) %collective-permute-start.2) | collective-permute-done | bytes 573472 | tf_op jit(solution)/shard_map/ppermute | solution.py:103
  21.6 2.2 %collective-permute-start.3 = (bf16[640,896]{1,0:T(8,128)(2,1)S(1)}, bf16[640,896]{1,0:T(8,128)(2,1)S(1)}, u32[]{:S(2)}, u32[]{:S(2)}) collective-permute-start(bf16[640,896]{1,0:T(8,128)(2,1)S(1)} %maximum_select_fusion.2), channel_id=1, source_target_pairs={{0,8},{16,24},{8,0},{24,16},{1,9},{17,25},{9,1},{25,17},{2,10},{18... | collective-permute-start | bytes 3440648 | tf_op jit(solution)/shard_map/ppermute | solution.py:127
  24.5 1.7 %collective-permute-done.5 = bf16[128,1280]{1,0:T(8,128)(2,1)} collective-permute-done((bf16[128,1280]{1,0:T(8,128)(2,1)}, bf16[128,1280]{1,0:T(8,128)(2,1)}, u32[]{:S(2)}, u32[]{:S(2)}) %collective-permute-start.5) | collective-permute-done | bytes 327712 | tf_op jit(solution)/shard_map/ppermute | solution.py:103
  26.2 1.7 %collective-permute-start.8 = (bf16[512,512]{1,0:T(8,128)(2,1)S(1)}, bf16[512,512]{1,0:T(8,128)(2,1)S(1)}, u32[]{:S(2)}, u32[]{:S(2)}) collective-permute-start(bf16[512,512]{1,0:T(8,128)(2,1)S(1)} %copy-done.8), channel_id=1, source_target_pairs={{0,4},{4,0},{1,5},{5,1},{2,6},{6,2},{3,7},{7,3},{8,12},{12,8},{9,1... | collective-permute-start | bytes 1572872 | tf_op jit(solution)/shard_map/ppermute | solution.py:103
  31.9 4.6 %collective-permute-done.6 = bf16[128,1280]{1,0:T(8,128)(2,1)S(1)} collective-permute-done((bf16[128,1280]{1,0:T(8,128)(2,1)}, bf16[128,1280]{1,0:T(8,128)(2,1)S(1)}, u32[]{:S(2)}, u32[]{:S(2)}) %collective-permute-start.6) | collective-permute-done | bytes 327712 | tf_op jit(solution)/shard_map/ppermute | solution.py:103
  44.7 3.5 %collective-permute-start.13 = (bf16[640,512]{1,0:T(8,128)(2,1)S(1)}, bf16[640,512]{1,0:T(8,128)(2,1)S(1)}, u32[]{:S(2)}, u32[]{:S(2)}) collective-permute-start(bf16[640,512]{1,0:T(8,128)(2,1)S(1)} %get-tuple-element.85), channel_id=1, source_target_pairs={{0,8},{24,16},{1,9},{25,17},{2,10},{26,18},{3,11},{27,19},{4,12},{... | collective-permute-start | bytes 1966088 | tf_op jit(solution)/shard_map/ppermute | solution.py:217
  54.3 4.1 %collective-permute-done.15 = bf16[128,1280]{1,0:T(8,128)(2,1)S(1)} collective-permute-done((bf16[128,1280]{1,0:T(8,128)(2,1)S(1)}, bf16[128,1280]{1,0:T(8,128)(2,1)S(1)}, u32[]{:S(2)}, u32[]{:S(2)}) %collective-permute-start.15) | collective-permute-done | bytes 327712 | tf_op jit(solution)/shard_map/ppermute | solution.py:103
  58.5 4.7 %collective-permute-start.19 = (bf16[640,512]{1,0:T(8,128)(2,1)S(1)}, bf16[640,512]{1,0:T(8,128)(2,1)S(1)}, u32[]{:S(2)}, u32[]{:S(2)}) collective-permute-start(bf16[640,512]{1,0:T(8,128)(2,1)S(1)} %get-tuple-element.52), channel_id=1, source_target_pairs={{0,8},{24,16},{1,9},{25,17},{2,10},{26,18},{3,11},{27,19},{4,12},{... | collective-permute-start | bytes 1966088 | tf_op jit(solution)/shard_map/ppermute | solution.py:217
  66.2 6.2 %collective-permute-start.21 = (bf16[1280,384]{1,0:T(8,128)(2,1)S(1)}, bf16[1280,384]{1,0:T(8,128)(2,1)S(1)}, u32[]{:S(2)}, u32[]{:S(2)}) collective-permute-start(bf16[1280,384]{1,0:T(8,128)(2,1)S(1)} %fusion.20), channel_id=1, source_target_pairs={{0,8},{24,16},{1,9},{25,17},{2,10},{26,18},{3,11},{27,19},{4,12},{... | collective-permute-start | bytes 2949128 | tf_op jit(solution)/shard_map/ppermute | solution.py:228
  83.6 13.4 %collective-permute-start.20 = (bf16[640,512]{1,0:T(8,128)(2,1)S(1)}, bf16[640,512]{1,0:T(8,128)(2,1)S(1)}, u32[]{:S(2)}, u32[]{:S(2)}) collective-permute-start(bf16[640,512]{1,0:T(8,128)(2,1)S(1)} %get-tuple-element.63), channel_id=1, source_target_pairs={{0,8},{16,24},{8,0},{24,16},{1,9},{17,25},{9,1},{25,17},{2,10},{18... | collective-permute-start | bytes 1966088 | tf_op jit(solution)/shard_map/ppermute | solution.py:217
  98.6 9.1 %collective-permute-done.14 = bf16[640,896]{1,0:T(8,128)(2,1)S(1)} collective-permute-done((bf16[640,896]{1,0:T(8,128)(2,1)S(1)}, bf16[640,896]{1,0:T(8,128)(2,1)S(1)}, u32[]{:S(2)}, u32[]{:S(2)}) %collective-permute-start.14) | collective-permute-done | bytes 1146912 | tf_op jit(solution)/shard_map/ppermute | solution.py:127
  108.9 1.6 %collective-permute-start.17 = (bf16[512,896]{1,0:T(8,128)(2,1)S(1)}, bf16[512,896]{1,0:T(8,128)(2,1)S(1)}, u32[]{:S(2)}, u32[]{:S(2)}) collective-permute-start(bf16[512,896]{1,0:T(8,128)(2,1)S(1)} %multiply_convert_fusion), channel_id=1, source_target_pairs={{0,4},{4,0},{1,5},{5,1},{2,6},{6,2},{3,7},{7,3},{8,12},{12,8},{9,1... | collective-permute-start | bytes 2752520 | tf_op jit(solution)/shard_map/ppermute | solution.py:103
  112.2 8.0 %collective-permute-start.24 = (bf16[640,384]{1,0:T(8,128)(2,1)S(1)}, bf16[640,384]{1,0:T(8,128)(2,1)S(1)}, u32[]{:S(2)}, u32[]{:S(2)}) collective-permute-start(bf16[640,384]{1,0:T(8,128)(2,1)S(1)} %get-tuple-element.65), channel_id=1, source_target_pairs={{0,8},{16,24},{8,0},{24,16},{1,9},{17,25},{9,1},{25,17},{2,10},{18... | collective-permute-start | bytes 1474568 | tf_op jit(solution)/shard_map/ppermute | solution.py:217
  122.4 1.6 %collective-permute-start.26 = (bf16[320,512]{1,0:T(8,128)(2,1)S(1)}, bf16[320,512]{1,0:T(8,128)(2,1)S(1)}, u32[]{:S(2)}, u32[]{:S(2)}) collective-permute-start(bf16[320,512]{1,0:T(8,128)(2,1)S(1)} %constant_dynamic-slice_fusion.1), channel_id=1, source_target_pairs={{0,4},{4,0},{1,5},{5,1},{2,6},{6,2},{3,7},{7,3},{8,12},{12,8},{9,1... | collective-permute-start | bytes 983048 | tf_op jit(solution)/shard_map/ppermute | solution.py:103
  124.1 7.2 %collective-permute-done.24 = bf16[640,384]{1,0:T(8,128)(2,1)S(1)} collective-permute-done((bf16[640,384]{1,0:T(8,128)(2,1)S(1)}, bf16[640,384]{1,0:T(8,128)(2,1)S(1)}, u32[]{:S(2)}, u32[]{:S(2)}) %collective-permute-start.24) | collective-permute-done | bytes 491552 | tf_op jit(solution)/shard_map/ppermute | solution.py:217
  132.7 1.6 %collective-permute-start.27 = (bf16[320,384]{1,0:T(8,128)(2,1)S(1)}, bf16[320,384]{1,0:T(8,128)(2,1)S(1)}, u32[]{:S(2)}, u32[]{:S(2)}) collective-permute-start(bf16[320,384]{1,0:T(8,128)(2,1)S(1)} %constant_dynamic-slice_fusion.2), channel_id=1, source_target_pairs={{0,4},{4,0},{1,5},{5,1},{2,6},{6,2},{3,7},{7,3},{8,12},{12,8},{9,1... | collective-permute-start | bytes 737288 | tf_op jit(solution)/shard_map/ppermute | solution.py:103
  134.2 3.4 %fusion.12 = (bf16[512,1792]{1,0:T(8,128)(2,1)}, bf16[512,1792]{1,0:T(8,128)(2,1)}) fusion(bf16[512,1792]{1,0:T(8,128)(2,1)S(1)} %copy-done.3, bf16[512,896]{1,0:T(8,128)(2,1)S(1)} %multiply_convert_fusion.1, bf16[512,896]{1,0:T(8,128)(2,1)S(1)} %collective-permute-done.17, pred[]{:T(512)S(6)} %eq.51, bf16[512,1792]{1,0:T(8,128)(2,1)S(1)} %copy-done.4), kind=kLoop, calls=%fused_computation.18 | loop fusion | flops 22937600 | bytes 9175041 | tf_op jit(solution)/shard_map/convert_element_type | solution.py:273
  139.2 2.3 %collective-permute-done.27 = bf16[320,384]{1,0:T(8,128)(2,1)S(1)} collective-permute-done((bf16[320,384]{1,0:T(8,128)(2,1)S(1)}, bf16[320,384]{1,0:T(8,128)(2,1)S(1)}, u32[]{:S(2)}, u32[]{:S(2)}) %collective-permute-start.27) | collective-permute-done | bytes 245792 | tf_op jit(solution)/shard_map/ppermute | solution.py:103
  146.1 2.6 %multiply_subtract_fusion = (f32[320,1792]{1,0:T(8,128)}, f32[320,1792]{1,0:T(8,128)}) fusion(f32[320,1792]{1,0:T(8,128)S(1)} %copy-done, f32[320]{0:T(512)S(1)} %minimum_reduce_fusion, bf16[320,384]{1,0:T(8,128)(2,1)S(1)} %get-tuple-element.75, bf16[320,512]{1,0:T(8,128)(2,1)S(1)} %get-tuple-element.73, bf16[320,384]{1,0:T(8,128)(2,1)S(1)} %collective-permute-done.27, ...), kind=kLoop, calls=%fused_computation.33 | loop fusion | flops 13189120 | bytes 10323201 | tf_op jit(solution)/shard_map/sub | solution.py:309
  (122 shorter events, 53.0 us)
Async XLA Ops:
  2.9 17.1 %collective-permute-start.2 = (bf16[320,896]{1,0:T(8,128)(2,1)}, bf16[320,896]{1,0:T(8,128)(2,1)}, u32[]{:S(2)}, u32[]{:S(2)}) collective-permute-start(bf16[320,896]{1,0:T(8,128)(2,1)} %dynamic-slice_convert_fusion.1), channel_id=1, source_target_pairs={{0,4},{4,0},{1,5},{5,1},{2,6},{6,2},{3,7},{7,3},{8,12},{12,8},{9,1... | collective-permute-start | bytes 1720328 | tf_op jit(solution)/shard_map/ppermute | solution.py:103
  5.9 23.6 %collective-permute-start = (bf16[128,2560]{1,0:T(8,128)(2,1)}, bf16[128,2560]{1,0:T(8,128)(2,1)}, u32[]{:S(2)}, u32[]{:S(2)}) collective-permute-start(bf16[128,2560]{1,0:T(8,128)(2,1)} %param.5), channel_id=1, source_target_pairs={{0,2},{2,0},{1,3},{3,1},{4,6},{6,4},{5,7},{7,5},{8,10},{10,8},{9,1... | collective-permute-start | bytes 1966088 | tf_op jit(solution)/shard_map/ppermute | solution.py:103
  14.3 11.9 %collective-permute-start.5 = (bf16[128,1280]{1,0:T(8,128)(2,1)}, bf16[128,1280]{1,0:T(8,128)(2,1)}, u32[]{:S(2)}, u32[]{:S(2)}) collective-permute-start(bf16[128,1280]{1,0:T(8,128)(2,1)} %get-tuple-element.42), channel_id=1, source_target_pairs={{0,4},{4,0},{1,5},{5,1},{2,6},{6,2},{3,7},{7,3},{8,12},{12,8},{9,1... | collective-permute-start | bytes 983048 | tf_op jit(solution)/shard_map/ppermute | solution.py:103
  21.6 26.6 %collective-permute-start.3 = (bf16[640,896]{1,0:T(8,128)(2,1)S(1)}, bf16[640,896]{1,0:T(8,128)(2,1)S(1)}, u32[]{:S(2)}, u32[]{:S(2)}) collective-permute-start(bf16[640,896]{1,0:T(8,128)(2,1)S(1)} %maximum_select_fusion.2), channel_id=1, source_target_pairs={{0,8},{16,24},{8,0},{24,16},{1,9},{17,25},{9,1},{25,17},{2,10},{18... | collective-permute-start | bytes 3440648 | tf_op jit(solution)/shard_map/ppermute | solution.py:127
  23.8 25.2 %collective-permute-start.4 = (bf16[640,896]{1,0:T(8,128)(2,1)S(1)}, bf16[640,896]{1,0:T(8,128)(2,1)S(1)}, u32[]{:S(2)}, u32[]{:S(2)}) collective-permute-start(bf16[640,896]{1,0:T(8,128)(2,1)S(1)} %maximum_select_fusion.2), channel_id=1, source_target_pairs={{8,16},{16,8},{9,17},{17,9},{10,18},{18,10},{11,19},{19,11},{12,20... | collective-permute-start | bytes 3440648 | tf_op jit(solution)/shard_map/ppermute | solution.py:127
  26.2 13.1 %collective-permute-start.8 = (bf16[512,512]{1,0:T(8,128)(2,1)S(1)}, bf16[512,512]{1,0:T(8,128)(2,1)S(1)}, u32[]{:S(2)}, u32[]{:S(2)}) collective-permute-start(bf16[512,512]{1,0:T(8,128)(2,1)S(1)} %copy-done.8), channel_id=1, source_target_pairs={{0,4},{4,0},{1,5},{5,1},{2,6},{6,2},{3,7},{7,3},{8,12},{12,8},{9,1... | collective-permute-start | bytes 1572872 | tf_op jit(solution)/shard_map/ppermute | solution.py:103
  30.6 11.4 %collective-permute-start.1 = (bf16[256,2560]{1,0:T(8,128)(2,1)S(1)}, bf16[256,2560]{1,0:T(8,128)(2,1)S(1)}, u32[]{:S(2)}, u32[]{:S(2)}) collective-permute-start(bf16[256,2560]{1,0:T(8,128)(2,1)S(1)} %pad_maximum_fusion), channel_id=1, source_target_pairs={{0,1},{1,0},{2,3},{3,2},{4,5},{5,4},{6,7},{7,6},{8,9},{9,8},{10,11... | collective-permute-start | bytes 3932168 | tf_op jit(solution)/shard_map/ppermute | solution.py:150
  39.3 11.0 %collective-permute-start.11 = (bf16[128,1280]{1,0:T(8,128)(2,1)S(1)}, bf16[128,1280]{1,0:T(8,128)(2,1)S(1)}, u32[]{:S(2)}, u32[]{:S(2)}) collective-permute-start(bf16[128,1280]{1,0:T(8,128)(2,1)S(1)} %copy-done.9), channel_id=1, source_target_pairs={{0,4},{4,0},{1,5},{5,1},{2,6},{6,2},{3,7},{7,3},{8,12},{12,8},{9,1... | collective-permute-start | bytes 983048 | tf_op jit(solution)/shard_map/ppermute | solution.py:103
  44.7 20.5 %collective-permute-start.13 = (bf16[640,512]{1,0:T(8,128)(2,1)S(1)}, bf16[640,512]{1,0:T(8,128)(2,1)S(1)}, u32[]{:S(2)}, u32[]{:S(2)}) collective-permute-start(bf16[640,512]{1,0:T(8,128)(2,1)S(1)} %get-tuple-element.85), channel_id=1, source_target_pairs={{0,8},{24,16},{1,9},{25,17},{2,10},{26,18},{3,11},{27,19},{4,12},{... | collective-permute-start | bytes 1966088 | tf_op jit(solution)/shard_map/ppermute | solution.py:217
  48.2 29.5 %collective-permute-start.10 = (bf16[640,896]{1,0:T(8,128)(2,1)S(1)}, bf16[640,896]{1,0:T(8,128)(2,1)S(1)}, u32[]{:S(2)}, u32[]{:S(2)}) collective-permute-start(bf16[640,896]{1,0:T(8,128)(2,1)S(1)} %collective-permute-done.3), channel_id=1, source_target_pairs={{8,16},{16,8},{9,17},{17,9},{10,18},{18,10},{11,19},{19,11},{12,20... | collective-permute-start | bytes 3440648 | tf_op jit(solution)/shard_map/ppermute | solution.py:127
  49.0 32.6 %collective-permute-start.9 = (bf16[640,896]{1,0:T(8,128)(2,1)S(1)}, bf16[640,896]{1,0:T(8,128)(2,1)S(1)}, u32[]{:S(2)}, u32[]{:S(2)}) collective-permute-start(bf16[640,896]{1,0:T(8,128)(2,1)S(1)} %collective-permute-done.4), channel_id=1, source_target_pairs={{16,24},{8,0},{17,25},{9,1},{18,26},{10,2},{19,27},{11,3},{20,28},... | collective-permute-start | bytes 3440648 | tf_op jit(solution)/shard_map/ppermute | solution.py:127
  52.8 10.6 %collective-permute-start.12 = (bf16[512,384]{1,0:T(8,128)(2,1)S(1)}, bf16[512,384]{1,0:T(8,128)(2,1)S(1)}, u32[]{:S(2)}, u32[]{:S(2)}) collective-permute-start(bf16[512,384]{1,0:T(8,128)(2,1)S(1)} %get-tuple-element.51), channel_id=1, source_target_pairs={{0,4},{4,0},{1,5},{5,1},{2,6},{6,2},{3,7},{7,3},{8,12},{12,8},{9,1... | collective-permute-start | bytes 1179656 | tf_op jit(solution)/shard_map/ppermute | solution.py:103
  58.5 21.5 %collective-permute-start.19 = (bf16[640,512]{1,0:T(8,128)(2,1)S(1)}, bf16[640,512]{1,0:T(8,128)(2,1)S(1)}, u32[]{:S(2)}, u32[]{:S(2)}) collective-permute-start(bf16[640,512]{1,0:T(8,128)(2,1)S(1)} %get-tuple-element.52), channel_id=1, source_target_pairs={{0,8},{24,16},{1,9},{25,17},{2,10},{26,18},{3,11},{27,19},{4,12},{... | collective-permute-start | bytes 1966088 | tf_op jit(solution)/shard_map/ppermute | solution.py:217
  65.5 14.5 %collective-permute-start.18 = (bf16[640,512]{1,0:T(8,128)(2,1)S(1)}, bf16[640,512]{1,0:T(8,128)(2,1)S(1)}, u32[]{:S(2)}, u32[]{:S(2)}) collective-permute-start(bf16[640,512]{1,0:T(8,128)(2,1)S(1)} %add_convert_fusion.3), channel_id=1, source_target_pairs={{8,16},{16,8},{9,17},{17,9},{10,18},{18,10},{11,19},{19,11},{12,20... | collective-permute-start | bytes 1966088 | tf_op jit(solution)/shard_map/ppermute | solution.py:217
  66.2 31.5 %collective-permute-start.21 = (bf16[1280,384]{1,0:T(8,128)(2,1)S(1)}, bf16[1280,384]{1,0:T(8,128)(2,1)S(1)}, u32[]{:S(2)}, u32[]{:S(2)}) collective-permute-start(bf16[1280,384]{1,0:T(8,128)(2,1)S(1)} %fusion.20), channel_id=1, source_target_pairs={{0,8},{24,16},{1,9},{25,17},{2,10},{26,18},{3,11},{27,19},{4,12},{... | collective-permute-start | bytes 2949128 | tf_op jit(solution)/shard_map/ppermute | solution.py:228
  77.7 30.0 %collective-permute-start.14 = (bf16[640,896]{1,0:T(8,128)(2,1)S(1)}, bf16[640,896]{1,0:T(8,128)(2,1)S(1)}, u32[]{:S(2)}, u32[]{:S(2)}) collective-permute-start(bf16[640,896]{1,0:T(8,128)(2,1)S(1)} %collective-permute-done.10), channel_id=1, source_target_pairs={{16,24},{8,0},{17,25},{9,1},{18,26},{10,2},{19,27},{11,3},{20,28},... | collective-permute-start | bytes 3440648 | tf_op jit(solution)/shard_map/ppermute | solution.py:127
  80.9 17.1 %collective-permute-start.22 = (bf16[640,512]{1,0:T(8,128)(2,1)S(1)}, bf16[640,512]{1,0:T(8,128)(2,1)S(1)}, u32[]{:S(2)}, u32[]{:S(2)}) collective-permute-start(bf16[640,512]{1,0:T(8,128)(2,1)S(1)} %get-tuple-element.61), channel_id=1, source_target_pairs={{8,16},{16,8},{9,17},{17,9},{10,18},{18,10},{11,19},{19,11},{12,20... | collective-permute-start | bytes 1966088 | tf_op jit(solution)/shard_map/ppermute | solution.py:217
  83.6 38.2 %collective-permute-start.20 = (bf16[640,512]{1,0:T(8,128)(2,1)S(1)}, bf16[640,512]{1,0:T(8,128)(2,1)S(1)}, u32[]{:S(2)}, u32[]{:S(2)}) collective-permute-start(bf16[640,512]{1,0:T(8,128)(2,1)S(1)} %get-tuple-element.63), channel_id=1, source_target_pairs={{0,8},{16,24},{8,0},{24,16},{1,9},{17,25},{9,1},{25,17},{2,10},{18... | collective-permute-start | bytes 1966088 | tf_op jit(solution)/shard_map/ppermute | solution.py:217
  97.9 13.6 %collective-permute-start.23 = (bf16[640,384]{1,0:T(8,128)(2,1)S(1)}, bf16[640,384]{1,0:T(8,128)(2,1)S(1)}, u32[]{:S(2)}, u32[]{:S(2)}) collective-permute-start(bf16[640,384]{1,0:T(8,128)(2,1)S(1)} %add_convert_fusion.6), channel_id=1, source_target_pairs={{8,16},{16,8},{9,17},{17,9},{10,18},{18,10},{11,19},{19,11},{12,20... | collective-permute-start | bytes 1474568 | tf_op jit(solution)/shard_map/ppermute | solution.py:217
  108.9 23.4 %collective-permute-start.17 = (bf16[512,896]{1,0:T(8,128)(2,1)S(1)}, bf16[512,896]{1,0:T(8,128)(2,1)S(1)}, u32[]{:S(2)}, u32[]{:S(2)}) collective-permute-start(bf16[512,896]{1,0:T(8,128)(2,1)S(1)} %multiply_convert_fusion), channel_id=1, source_target_pairs={{0,4},{4,0},{1,5},{5,1},{2,6},{6,2},{3,7},{7,3},{8,12},{12,8},{9,1... | collective-permute-start | bytes 2752520 | tf_op jit(solution)/shard_map/ppermute | solution.py:103
  112.2 19.1 %collective-permute-start.24 = (bf16[640,384]{1,0:T(8,128)(2,1)S(1)}, bf16[640,384]{1,0:T(8,128)(2,1)S(1)}, u32[]{:S(2)}, u32[]{:S(2)}) collective-permute-start(bf16[640,384]{1,0:T(8,128)(2,1)S(1)} %get-tuple-element.65), channel_id=1, source_target_pairs={{0,8},{16,24},{8,0},{24,16},{1,9},{17,25},{9,1},{25,17},{2,10},{18... | collective-permute-start | bytes 1474568 | tf_op jit(solution)/shard_map/ppermute | solution.py:217
  120.2 12.1 %collective-permute-start.25 = (bf16[640,384]{1,0:T(8,128)(2,1)S(1)}, bf16[640,384]{1,0:T(8,128)(2,1)S(1)}, u32[]{:S(2)}, u32[]{:S(2)}) collective-permute-start(bf16[640,384]{1,0:T(8,128)(2,1)S(1)} %get-tuple-element.66), channel_id=1, source_target_pairs={{8,16},{16,8},{9,17},{17,9},{10,18},{18,10},{11,19},{19,11},{12,20... | collective-permute-start | bytes 1474568 | tf_op jit(solution)/shard_map/ppermute | solution.py:217
  122.4 16.5 %collective-permute-start.26 = (bf16[320,512]{1,0:T(8,128)(2,1)S(1)}, bf16[320,512]{1,0:T(8,128)(2,1)S(1)}, u32[]{:S(2)}, u32[]{:S(2)}) collective-permute-start(bf16[320,512]{1,0:T(8,128)(2,1)S(1)} %constant_dynamic-slice_fusion.1), channel_id=1, source_target_pairs={{0,4},{4,0},{1,5},{5,1},{2,6},{6,2},{3,7},{7,3},{8,12},{12,8},{9,1... | collective-permute-start | bytes 983048 | tf_op jit(solution)/shard_map/ppermute | solution.py:103
  132.7 8.9 %collective-permute-start.27 = (bf16[320,384]{1,0:T(8,128)(2,1)S(1)}, bf16[320,384]{1,0:T(8,128)(2,1)S(1)}, u32[]{:S(2)}, u32[]{:S(2)}) collective-permute-start(bf16[320,384]{1,0:T(8,128)(2,1)S(1)} %constant_dynamic-slice_fusion.2), channel_id=1, source_target_pairs={{0,4},{4,0},{1,5},{5,1},{2,6},{6,2},{3,7},{7,3},{8,12},{12,8},{9,1... | collective-permute-start | bytes 737288 | tf_op jit(solution)/shard_map/ppermute | solution.py:103
  (17 other events, 117.4 us)
